TPU v7x, 256 devices: a whole 4x4x8 slice. The times are simulated.
256 devices in a mesh: stn: 16 (over z_hi, x, core), tm: 16 (over z_lo, y).
Axes of the slice: x: 4, y: 4, z: 8 (z_hi: 2, z_lo: 4; z = z_hi * 4 + z_lo), core: 2. Of those that a mesh axis runs over, the one named last changes fastest.
Arguments:
- volts: bfloat16 [256, 1048576], P('stn', 'tm'), may hold values from -8 to 8
- taps: float32 [12, 2048], replicated, may hold values from -1.75 to 1.75
- tile_pairs: int32 [3, 2], replicated, may hold values from 0 to 1, as said below
Outputs:
- visibility: float32 [2, 1024, 3, 128, 128], P(None, ('stn', 'tm'))
Inputs may be any that keep to these rules, and one draw needn't show every extreme that they name: `tile_pairs`: every pair (a, b) with a <= b < 2 appears exactly once, a first, in an order drawn from the seed.
All inputs are finite; a program needn't handle non-finite values.
Results may differ from a plain program's by a relative error of at most 0.0018.
Values may be sent and summed in bfloat16 or wider, within the bound.
No kernel may reach another device: no remote copies, remote signals or barrier semaphores. Data moves between devices by JAX's collectives and lax.ppermute only.
A program may use at most 128 MiB of HBM per device.

v0:
```python
import math

import jax
import jax.numpy as jnp
from jax import lax
from jax.sharding import PartitionSpec as P

TILE = 128


def passed_along(array, axis, by):
    peers = lax.axis_size(axis)
    pairs = [(i, i + by) for i in range(peers) if 0 <= i + by < peers]
    return lax.ppermute(array, axis, pairs)


def tile_grams(stacked, tile_pairs):
    real_parts = []
    imag_parts = []
    for number in range(tile_pairs.shape[0]):
        left_rows = lax.dynamic_slice_in_dim(stacked, tile_pairs[number, 0] * TILE, TILE, 2)
        right_rows = lax.dynamic_slice_in_dim(stacked, tile_pairs[number, 1] * TILE, TILE, 2)
        real_parts.append(
            jnp.einsum("cpis,cpjs->cij", left_rows, right_rows, preferred_element_type=jnp.float32)
        )
        cross_one = jnp.einsum(
            "cis,cjs->cij", left_rows[:, 1], right_rows[:, 0], preferred_element_type=jnp.float32
        )
        cross_two = jnp.einsum(
            "cis,cjs->cij", left_rows[:, 0], right_rows[:, 1], preferred_element_type=jnp.float32
        )
        imag_parts.append(cross_one - cross_two)
    return jnp.stack([jnp.stack(real_parts, 1), jnp.stack(imag_parts, 1)], 0)


def angle_table(rows, cols, modulus):
    row_idx = lax.broadcasted_iota(jnp.int32, (rows, cols), 0)
    col_idx = lax.broadcasted_iota(jnp.int32, (rows, cols), 1)
    return (row_idx * col_idx % modulus).astype(jnp.float32) * (2.0 * math.pi / modulus)


def transform_channels(filtered, fft_len):
    local_inputs, spectra_dev = (filtered.shape[0], filtered.shape[1])
    first_len = 2 ** ((fft_len.bit_length() - 1) // 2)
    second_len = fft_len // first_len
    half_second = second_len // 2
    high = lax.Precision.HIGHEST
    samples = filtered.reshape(local_inputs, spectra_dev, first_len, second_len)
    first_angle = angle_table(first_len, first_len, first_len)
    first_cos = jnp.cos(first_angle)
    first_sin = jnp.sin(first_angle)
    section_re = jnp.einsum(
        "isab,ak->iskb", samples, first_cos, precision=high, preferred_element_type=jnp.float32
    )
    section_im = -jnp.einsum(
        "isab,ak->iskb", samples, first_sin, precision=high, preferred_element_type=jnp.float32
    )
    twiddle = angle_table(first_len, second_len, fft_len)
    twiddle_cos = jnp.cos(twiddle)
    twiddle_sin = jnp.sin(twiddle)
    turned_re = section_re * twiddle_cos + section_im * twiddle_sin
    turned_im = section_im * twiddle_cos - section_re * twiddle_sin
    second_angle = angle_table(second_len, half_second, second_len)
    norming = 1.0 / math.sqrt(fft_len)
    second_cos = jnp.cos(second_angle) * norming
    second_sin = jnp.sin(second_angle) * norming
    out_re = jnp.einsum(
        "iskb,bq->qkis", turned_re, second_cos, precision=high, preferred_element_type=jnp.float32
    ) + jnp.einsum(
        "iskb,bq->qkis", turned_im, second_sin, precision=high, preferred_element_type=jnp.float32
    )
    out_im = jnp.einsum(
        "iskb,bq->qkis", turned_im, second_cos, precision=high, preferred_element_type=jnp.float32
    ) - jnp.einsum(
        "iskb,bq->qkis", turned_re, second_sin, precision=high, preferred_element_type=jnp.float32
    )
    chan_count = fft_len // 2
    both = jnp.stack(
        [
            out_re.reshape(chan_count, local_inputs, spectra_dev),
            out_im.reshape(chan_count, local_inputs, spectra_dev),
        ],
        axis=1,
    )
    return both.astype(jnp.bfloat16)


def shards(volts, taps, tile_pairs):
    local_inputs, local_samples = volts.shape
    tap_count, fft_len = taps.shape
    spectra_dev = local_samples // fft_len
    frames = volts.reshape(local_inputs, spectra_dev, fft_len)
    earlier = passed_along(frames[:, spectra_dev - (tap_count - 1) :, :], "tm", 1)
    padded = jnp.concatenate([earlier, frames], axis=1)
    filtered = jnp.zeros((local_inputs, spectra_dev, fft_len), jnp.float32)
    for step in range(tap_count):
        filtered = filtered + padded[:, step : step + spectra_dev].astype(jnp.float32) * taps[step]
    spectra = transform_channels(filtered, fft_len)
    tm_count = lax.axis_size("tm")
    total_spectra = spectra_dev * tm_count
    turned = lax.all_to_all(spectra, "stn", split_axis=0, concat_axis=2, tiled=True)
    regrouped = lax.all_to_all(turned, "tm", split_axis=0, concat_axis=3, tiled=True)
    return tile_grams(regrouped, tile_pairs) / jnp.float32(total_spectra)


def solution(mesh):
    return jax.shard_map(
        shards,
        mesh=mesh,
        in_specs=(P("stn", "tm"), P(), P()),
        out_specs=P(None, ("stn", "tm"), None, None, None),
        check_vma=False,
    )
```

profile of v0, /device:TPU:64, one launch (start us, length us, event | category | flops | bytes accessed | tf_op | source)
XLA Modules:
  0.0 422.6 jit_solution(17203266332861405256)
XLA Ops:
  0.0 0.0 copy-start.3
  0.0 2.8 copy.95
  2.8 0.3 slice.168
  3.1 0.4 copy.54
  3.5 3.5 collective-permute-start
  7.0 0.1 fusion.64
  7.1 0.0 copy-done.3
  7.1 0.1 fusion.113
  7.2 18.2 %collective-permute-done = bf16[16,11,2048]{2,0,1:T(8,128)(2,1)S(1)} collective-permute-done((bf16[16,11,2048]{2,0,1:T(8,128)(2,1)S(1)}, bf16[16,11,2048]{2,0,1:T(8,128)(2,1)S(1)}, u32[]{:S(2)}, u32[]{:S(2)}) %collective-permute-start) | collective-permute-done | bytes 720928 | tf_op jit(solution)/shard_map/ppermute | solution.py:14
  25.4 0.4 copy.55
  25.8 9.1 %multiply_add_fusion.1 = f32[16,32,2048]{2,1,0:T(8,128)} fusion(bf16[16,32,2048]{2,1,0:T(8,128)(2,1)S(1)} %bitcast.163, bf16[16,11,2048]{2,1,0:T(8,128)(2,1)S(1)} %copy.55, f32[2048]{0:T(1024)S(1)} %bitcast.176, f32[2048]{0:T(1024)S(1)} %bitcast.177, f32[2048]{0:T(1024)S(1)} %bitcast.167, f32[2048]{0:T(1024)S(1)} %bitcast.168, f32[2048]{0:T(1024)S(1)} %bitcast.169, ...), kind=kLoop, calls=%fused_computation.34 | loop fusion | flops 71303168 | bytes 7110656 | tf_op jit(solution)/shard_map/add | solution.py:97
  34.9 7.8 %reshape.57 = f32[16,32,32,64]{3,2,1,0:T(8,128)} reshape(f32[16,32,2048]{2,1,0:T(8,128)} %multiply_add_fusion.1) | data formatting | bytes 8388608 | tf_op jit(solution)/shard_map/reshape | solution.py:48
  42.7 0.0 copy-start.2
  42.7 11.2 %fusion.45 = f32[32,16,32,64]{3,0,2,1:T(8,128)S(1)} fusion(f32[16,32,32,64]{3,2,1,0:T(8,128)} %reshape.57), kind=kOutput, calls=%fused_computation.98 | convolution fusion | flops 402667520 | bytes 8388608 | tf_op jit(solution)/shard_map/isab,ak->iskb/dot_general | solution.py:55
  54.0 0.0 copy-done.2
  54.0 0.0 copy-start
  54.0 8.3 %fusion.47 = f32[32,16,32,64]{3,0,2,1:T(8,128)S(1)} fusion(f32[16,32,32,64]{3,2,1,0:T(8,128)S(1)} %copy-done.2), kind=kOutput, calls=%fused_computation.100 | convolution fusion | flops 402667520 | bytes 8388608 | tf_op jit(solution)/shard_map/isab,ak->iskb/dot_general | solution.py:52
  62.2 0.0 copy-start.1
  62.3 40.4 %fusion.2 = f32[32,16,32,32]{3,0,2,1:T(8,128)} fusion(f32[32,16,32,64]{3,0,2,1:T(8,128)S(1)} %fusion.47, f32[32,16,32,64]{3,0,2,1:T(8,128)S(1)} %fusion.45, f32[32,64]{1,0:T(8,128)S(1)} %get-tuple-element.23, f32[32,64]{1,0:T(8,128)S(1)} %get-tuple-element.24), kind=kOutput, calls=%fused_computation.12 | convolution fusion | flops 406878208 | bytes 10502144 | tf_op jit(solution)/shard_map/iskb,bq->qkis/dot_general | solution.py:69
  102.7 40.6 %fusion = f32[32,16,32,32]{3,0,2,1:T(8,128)} fusion(f32[32,16,32,64]{3,0,2,1:T(8,128)S(1)} %fusion.47, f32[32,16,32,64]{3,0,2,1:T(8,128)S(1)} %fusion.45, f32[32,64]{1,0:T(8,128)S(1)} %get-tuple-element.23, f32[32,64]{1,0:T(8,128)S(1)} %get-tuple-element.24), kind=kOutput, calls=%fused_computation.10 | convolution fusion | flops 406878208 | bytes 10502144 | tf_op jit(solution)/shard_map/iskb,bq->qkis/dot_general | solution.py:72
  143.3 0.0 copy-done
  143.3 0.0 copy-done.1
  143.3 42.0 %fusion.8 = bf16[32,32,16,32]{1,0,3,2:T(8,128)(2,1)} fusion(f32[32,16,32,32]{3,0,2,1:T(8,128)} %fusion.2, f32[32,16,32,64]{3,0,2,1:T(8,128)S(1)} %fusion.47, f32[32,16,32,64]{3,0,2,1:T(8,128)S(1)} %fusion.45, f32[32,64]{1,0:T(8,128)S(1)} %get-tuple-element.23, f32[32,64]{1,0:T(8,128)S(1)} %get-tuple-element.24), kind=kOutput, calls=%fused_computation.32 | convolution fusion | flops 407926784 | bytes 11550720 | tf_op jit(solution)/shard_map/iskb,bq->qkis/dot_general | solution.py:67
  185.3 6.2 %stack_reshape.8 = bf16[1024,1,16,32]{0,3,2,1:T(8,128)(2,1)S(1)} reshape(bf16[32,32,16,32]{1,0,3,2:T(8,128)(2,1)} %fusion.8) | data formatting | bytes 2097152 | tf_op jit(solution)/shard_map/stack;reshape | solution.py:78
  191.4 44.5 %fusion.9 = bf16[32,32,16,32]{1,0,3,2:T(8,128)(2,1)} fusion(f32[32,16,32,32]{3,0,2,1:T(8,128)} %fusion, f32[32,16,32,64]{3,0,2,1:T(8,128)} %copy-done.1, f32[32,16,32,64]{3,0,2,1:T(8,128)} %copy-done, f32[32,64]{1,0:T(8,128)S(1)} %get-tuple-element.23, f32[32,64]{1,0:T(8,128)S(1)} %get-tuple-element.24), kind=kOutput, calls=%fused_computation.33 | convolution fusion | flops 407926784 | bytes 11550720 | tf_op jit(solution)/shard_map/iskb,bq->qkis/dot_general | solution.py:74
  235.9 7.2 %stack_reshape.9 = bf16[1024,1,16,32]{0,3,2,1:T(8,128)(2,1)} reshape(bf16[32,32,16,32]{1,0,3,2:T(8,128)(2,1)} %fusion.9) | data formatting | bytes 2097152 | tf_op jit(solution)/shard_map/stack;reshape | solution.py:78
  243.1 1.4 pad_maximum_fusion.1
  244.6 12.1 %copy.56 = bf16[1024,2,16,32]{3,2,1,0:T(8,128)(2,1)} copy(bf16[1024,2,16,32]{0,3,2,1:T(8,128)(2,1)S(1)} %pad_maximum_fusion.1) | data formatting | bytes 4194304 | tf_op jit(solution)/shard_map/stack | solution.py:78
  256.7 13.4 %reshape.65 = bf16[16,2,32768]{2,1,0:T(2,128)(2,1)S(1)} reshape(bf16[1024,2,16,32]{3,2,1,0:T(8,128)(2,1)} %copy.56) | data formatting | bytes 4194304
  270.1 61.1 %all_to_all.36 = bf16[16,2,32768]{2,1,0:T(2,128)(2,1)} all-to-all(bf16[16,2,32768]{2,1,0:T(2,128)(2,1)S(1)} %reshape.65), channel_id=1, replica_groups=mesh['stn'=16,'tm'=16] {'stn'}, dimensions={0} | all-to-all | bytes 4194304 | tf_op jit(solution)/shard_map/all_to_all | solution.py:101
  331.2 12.9 %reshape.66 = bf16[1024,2,16,32]{3,2,1,0:T(8,128)(2,1)} reshape(bf16[16,2,32768]{2,1,0:T(2,128)(2,1)} %all_to_all.36) | data formatting | bytes 4194304
  344.2 10.2 %copy.58 = bf16[64,2,16,16,32]{0,4,3,2,1:T(8,128)(2,1)} copy(bf16[64,2,16,16,32]{4,3,1,0,2:T(8,128)(2,1)} %bitcast.151) | data formatting | bytes 4194304 | tf_op jit(solution)/shard_map/all_to_all | solution.py:101
  354.4 0.0 copy-start.4
  354.4 7.8 %copy.59 = bf16[64,2,256,32]{2,3,1,0:T(8,128)(2,1)} copy(bf16[64,2,256,32]{0,3,2,1:T(8,128)(2,1)} %bitcast.161) | data formatting | bytes 4194304 | tf_op jit(solution)/shard_map/all_to_all | solution.py:101
  362.2 6.8 %all-to-all-start.1 = ((bf16[64,2,256,32]{2,3,1,0:T(8,128)(2,1)}), bf16[64,2,256,32]{2,3,1,0:T(8,128)(2,1)S(1)}, u32[]{:S(2)}, u32[]{:S(2)}) async-start(bf16[64,2,256,32]{2,3,1,0:T(8,128)(2,1)} %copy.59), calls=%async_computation.1 | async-start | bytes 4194304 | tf_op jit(solution)/shard_map/all_to_all | solution.py:102
  369.0 0.0 copy-done.4
  369.0 0.6 fusion.114
  373.3 43.5 %all-to-all-done.1 = bf16[64,2,256,32]{2,3,1,0:T(8,128)(2,1)S(1)} async-done(((bf16[64,2,256,32]{2,3,1,0:T(8,128)(2,1)}), bf16[64,2,256,32]{2,3,1,0:T(8,128)(2,1)S(1)}, u32[]{:S(2)}, u32[]{:S(2)}) %all-to-all-start.1) | async-done | bytes 2097184 | tf_op jit(solution)/shard_map/all_to_all | solution.py:102
  416.8 0.2 copy.60
  417.0 0.5 convolution_bitcast_fusion.2
  417.5 0.4 fusion.35
  417.8 0.5 convolution_bitcast_fusion.1
  418.3 0.3 fusion.34
  418.7 0.5 convolution_bitcast_fusion
  419.1 0.3 fusion.33
  419.5 0.4 fusion.26
  419.9 0.4 fusion.25
  420.2 0.4 fusion.24
  420.6 0.1 maximum_bitcast_fusion
  420.6 0.1 maximum_bitcast_fusion.1
  420.7 0.2 maximum_multiply_fusion
  420.9 1.3 copy.67
Async XLA Ops:
  0.0 7.1 %copy-start.3 = (f32[12,2048]{1,0:T(8,128)S(1)}, f32[12,2048]{1,0:T(8,128)}, u32[]{:S(2)}) copy-start(f32[12,2048]{1,0:T(8,128)} %param.4) | copy-start | bytes 294916
  3.5 21.9 %collective-permute-start = (bf16[16,11,2048]{2,0,1:T(8,128)(2,1)S(1)}, bf16[16,11,2048]{2,0,1:T(8,128)(2,1)S(1)}, u32[]{:S(2)}, u32[]{:S(2)}) collective-permute-start(bf16[16,11,2048]{2,0,1:T(8,128)(2,1)S(1)} %copy.54), channel_id=1, source_target_pairs={{0,1},{1,2},{2,3},{3,4},{4,5},{5,6},{6,7},{7,8},{8,9},{9,10},{10,1... | collective-permute-start | bytes 2162696 | tf_op jit(solution)/shard_map/ppermute | solution.py:14
  42.7 11.2 %copy-start.2 = (f32[16,32,32,64]{3,2,1,0:T(8,128)S(1)}, f32[16,32,32,64]{3,2,1,0:T(8,128)}, u32[]{:S(2)}) copy-start(f32[16,32,32,64]{3,2,1,0:T(8,128)} %reshape.57) | copy-start | bytes 12582916
  54.0 89.3 %copy-start = (f32[32,16,32,64]{3,0,2,1:T(8,128)}, f32[32,16,32,64]{3,0,2,1:T(8,128)S(1)}, u32[]{:S(2)}) copy-start(f32[32,16,32,64]{3,0,2,1:T(8,128)S(1)} %fusion.45) | copy-start | bytes 12582916
  62.2 81.0 %copy-start.1 = (f32[32,16,32,64]{3,0,2,1:T(8,128)}, f32[32,16,32,64]{3,0,2,1:T(8,128)S(1)}, u32[]{:S(2)}) copy-start(f32[32,16,32,64]{3,0,2,1:T(8,128)S(1)} %fusion.47) | copy-start | bytes 12582916
  354.4 14.6 %copy-start.4 = (s32[3,2]{0,1:T(2,128)S(1)}, s32[3,2]{0,1:T(2,128)}, u32[]{:S(2)}) copy-start(s32[3,2]{0,1:T(2,128)} %param.5) | copy-start | bytes 76
  362.2 54.6 %all-to-all-start.1 = ((bf16[64,2,256,32]{2,3,1,0:T(8,128)(2,1)}), bf16[64,2,256,32]{2,3,1,0:T(8,128)(2,1)S(1)}, u32[]{:S(2)}, u32[]{:S(2)}) async-start(bf16[64,2,256,32]{2,3,1,0:T(8,128)(2,1)} %copy.59), calls=%async_computation.1 | async-start | bytes 4194304 | tf_op jit(solution)/shard_map/all_to_all | solution.py:102
where the time goes:
time: 430 us; the launch traced here: 423 us
  matrix products  191 us (44%)
  local copies, waits for them, and re-layouts  83.8 us (19%)
  waiting for transfers between devices  61.7 us (14%)
  blocking collectives  61.1 us (14%)
  other arithmetic  10.8 us (3%)
  starting transfers between devices  10.3 us (2%)
  between operations  4.35 us (1%)
    all_to_all x1, blocking collectives, shards(): lax.all_to_all(spectra, 'stn', split_axis=0, concat_axis=2, tiled=True)  61.1 us
    dot_general x1, matrix products, transform_channels(): jnp.einsum('iskb,bq->qkis', turned_re, second_sin, precision=high, prefer...  44.5 us
    all_to_all x1, waiting for transfers between devices, shards(): lax.all_to_all(turned, 'tm', split_axis=0, concat_axis=3, tiled=True)  43.5 us
    dot_general x1, matrix products, transform_channels(): jnp.einsum('iskb,bq->qkis', turned_re, second_cos, precision=high, prefer...  42 us
    dot_general x1, matrix products, transform_channels(): jnp.einsum('iskb,bq->qkis', turned_im, second_cos, precision=high, prefer...  40.6 us
    dot_general x1, matrix products, transform_channels(): jnp.einsum('iskb,bq->qkis', turned_im, second_sin, precision=high, prefer...  40.4 us
    unnamed x13, local copies, waits for them, and re-layouts  29.2 us
    another operation x3, local copies, waits for them, and re-layouts, transform_channels(): jnp.stack([out_re.reshape(chan_count, local_inputs, spectra_dev), out_im....  25.5 us
  transfers between devices with their start and end apart: 2, of which 2 were waited for; matrix products, arithmetic and copies ran while one was open for 0% of the time, Pallas kernels for 0%

commit v1 on v0

v1 whole, which is shorter than its diff:
```python
import functools
import math

import jax
import jax.numpy as jnp
import ml_dtypes
import numpy as np
from jax import lax
from jax.experimental import pallas as pl
from jax.experimental.pallas import tpu as pltpu
from jax.sharding import PartitionSpec as P

TILE = 128
LANES = 128
RADIX = 16
BACK = 5
BLOCK = 2
HALF = 16
VMEM_LIMIT = 48 * 1024 * 1024


def second_step_table(fft_len):
    length = fft_len // RADIX
    quarter = length // 2
    place = np.arange(length, dtype=np.int64)
    out = np.zeros((RADIX // 2, 2 * length, 2 * length), np.float64)

    def rows(kappa):
        chan = kappa + RADIX * np.arange(quarter, dtype=np.int64)
        angle = 2.0 * np.pi * ((chan[:, None] * place[None, :]) % fft_len) / fft_len
        return np.cos(angle), np.sin(angle)

    for pair in range(RADIX // 2):
        for slot in range(2):
            if pair == 0:
                kappa = 0 if slot == 0 else RADIX // 2
            else:
                kappa = pair if slot == 0 else RADIX - pair
            cos, sin = rows(kappa)
            first = slot * length
            if pair == 0:
                cols = slice(slot * length, (slot + 1) * length)
                out[pair, first : first + quarter, cols] = cos
                out[pair, first + quarter : first + length, cols] = -sin
            else:
                sign = 1.0 if slot == 0 else -1.0
                out[pair, first : first + quarter, :length] = cos
                out[pair, first : first + quarter, length:] = -sign * sin
                out[pair, first + quarter : first + length, :length] = -sin
                out[pair, first + quarter : first + length, length:] = -sign * cos
    out = (out / math.sqrt(fft_len)).astype(np.float32)
    high = out.astype(ml_dtypes.bfloat16)
    low = (out - high.astype(np.float32)).astype(ml_dtypes.bfloat16)
    return np.concatenate([high, low], axis=1)


def first_step(x):
    c1, c2, c3 = (math.cos(math.pi * j / 8) for j in (1, 2, 3))
    a = [x[n] + x[n + 8] for n in range(8)]
    b = [x[n] - x[n + 8] for n in range(8)]
    d = [None] + [b[n] - b[8 - n] for n in (1, 2, 3)]
    s = [None] + [b[n] + b[8 - n] for n in (1, 2, 3)]
    u, v = b[0] + c2 * d[2], b[0] - c2 * d[2]
    p, q = c1 * d[1] + c3 * d[3], c3 * d[1] - c1 * d[3]
    g, h = b[4] + c2 * s[2], b[4] - c2 * s[2]
    m, n = c3 * s[1] + c1 * s[3], c1 * s[1] - c3 * s[3]
    e = [a[n_] + a[n_ + 4] for n_ in range(4)]
    f = [a[n_] - a[n_ + 4] for n_ in range(4)]
    w, z = c2 * (f[1] - f[3]), c2 * (f[1] + f[3])
    even, odd = e[0] + e[2], e[1] + e[3]
    return [
        (even + odd, even - odd),
        (u + p, g + m),
        (f[0] + w, f[2] + z),
        (v + q, n - h),
        (e[0] - e[2], e[1] - e[3]),
        (v - q, h + n),
        (f[0] - w, z - f[2]),
        (u - p, m - g),
    ]


def spectra_kernel(plan, fft_len, keep_ref, *refs):
    source_count = 1 + max(src for taps in plan for src, _, _ in taps)
    sources = refs[:source_count]
    taps_ref, table_ref = refs[source_count : source_count + 2]
    out_ref, filt, high, low, turned = refs[-5:]
    rows = sources[0].shape[0]
    outputs = len(plan)
    tap_count = taps_ref.shape[0]
    keep = keep_ref[0] != 0

    @pl.loop(0, RADIX)
    def _(col):
        base = pl.multiple_of(col * LANES, LANES)
        weights = [
            jnp.broadcast_to(taps_ref[pl.ds(j, 1), pl.ds(base, LANES)], (rows, LANES)) for j in range(tap_count)
        ]
        for block in range(0, outputs, BLOCK):
            held = {}
            for out in range(block, block + BLOCK):
                sums = {False: None, True: None}
                for j, (src, frame, wiped) in enumerate(plan[out]):
                    if (src, frame) not in held:
                        lane = pl.multiple_of(frame * fft_len + base, LANES)
                        held[src, frame] = sources[src][:, pl.ds(lane, LANES)].astype(jnp.float32)
                    term = held[src, frame] * weights[j]
                    sums[wiped] = term if sums[wiped] is None else sums[wiped] + term
                total = sums[False]
                if sums[True] is not None:
                    total = total + jnp.where(keep, sums[True], 0.0)
                filt[pl.ds(out * rows, rows), pl.ds(base, LANES)] = total

    @pl.loop(0, outputs)
    def _(out):
        at = pl.ds(pl.multiple_of(out * rows, rows), rows)
        parts = first_step([filt[at, n * LANES : (n + 1) * LANES] for n in range(RADIX)])
        for pair, halves in enumerate(parts):
            for k, value in enumerate(halves):
                top = value.astype(jnp.bfloat16)
                high[pair, at, k * LANES : (k + 1) * LANES] = top
                low[pair, at, k * LANES : (k + 1) * LANES] = (value - top.astype(jnp.float32)).astype(jnp.bfloat16)

    quarter = fft_len // RADIX // 2
    per_dev = 4
    spread = RADIX // per_dev * 2 * per_dev

    def product(left, right):
        return lax.dot_general(left, right, (((1,), (1,)), ((), ())), preferred_element_type=jnp.float32)

    size = 2 * LANES
    for pair in range(RADIX // 2):
        table_high, table_low = table_ref[pair, :size], table_ref[pair, size:]
        result = (
            product(table_high, low[pair]) + product(table_low, high[pair])
        ) + product(table_high, high[pair])
        for slot in range(2):
            kappa = (pair, RADIX - pair)[slot] if pair else (0, RADIX // 2)[slot]
            for part in range(2):
                first = slot * LANES + part * quarter
                row = (kappa // per_dev) * 2 * per_dev + (kappa % per_dev) * 2 + part
                for lane in range(result.shape[1] // LANES):
                    turned[lane, pl.ds(row, quarter, stride=spread), :] = result[
                        first : first + quarter, lane * LANES : (lane + 1) * LANES
                    ]
    for lane in range(turned.shape[0]):
        out_ref[:, lane * LANES : (lane + 1) * LANES] = turned[lane].astype(jnp.bfloat16)


def spectra_call(plan, sources, taps, table, keep, half, previous):
    rows = sources[0].shape[0]
    fft_len = taps.shape[1]
    cols = len(plan) * rows
    vmem = pl.BlockSpec(memory_space=pltpu.VMEM)
    operands = [keep, *sources, taps, table]
    in_specs = [pl.BlockSpec(memory_space=pltpu.SMEM)] + [vmem] * (len(operands) - 1)
    aliases = {}
    if previous is not None:
        aliases = {len(operands): 0}
        operands.append(previous)
        in_specs.append(pl.BlockSpec(memory_space=pl.ANY))
    return pl.pallas_call(
        functools.partial(spectra_kernel, plan, fft_len),
        grid=(1,),
        out_shape=jax.ShapeDtypeStruct((fft_len, 2 * cols), jnp.bfloat16),
        in_specs=in_specs,
        out_specs=pl.BlockSpec((fft_len, cols), lambda i: (0, half)),
        scratch_shapes=[
            pltpu.VMEM((cols, fft_len), jnp.float32),
            pltpu.VMEM((RADIX // 2, cols, 2 * LANES), jnp.bfloat16),
            pltpu.VMEM((RADIX // 2, cols, 2 * LANES), jnp.bfloat16),
            pltpu.VMEM((cols // LANES, fft_len, LANES), jnp.float32),
        ],
        input_output_aliases=aliases,
        compiler_params=pltpu.CompilerParams(vmem_limit_bytes=VMEM_LIMIT),
        cost_estimate=pl.CostEstimate(flops=10**9, bytes_accessed=6 * 2**20, transcendentals=0),
        name="spectra%d" % half,
    )(*operands)


def gram_kernel(scale, pairs_ref, got_ref, out_ref, wide, left, right):
    groups = wide.shape[0]
    stations = 16
    times = 16
    chans = out_ref.shape[1]
    per_src = 2 * chans
    inputs = LANES // 8
    for group in range(groups):
        wide[group] = got_ref[:, group * LANES : (group + 1) * LANES].astype(jnp.float32)

    @pl.loop(0, stations)
    def _(stn):
        at = pl.ds(pl.multiple_of(stn * inputs, inputs), inputs)
        first = pl.multiple_of(stn * times * per_src, times * per_src)
        for chan in range(chans):
            parts = [
                [wide[group, pl.ds(first + chan * 2 + part, times, stride=per_src), :] for group in range(groups)]
                for part in range(2)
            ]
            plain = jnp.concatenate(parts[0] + parts[1], 0).T.astype(jnp.bfloat16)
            turned = jnp.concatenate([-v for v in parts[1]] + parts[0], 0).T.astype(jnp.bfloat16)
            for t in range(LANES // inputs):
                cols = slice(t * LANES, (t + 1) * LANES)
                left[chan, at, cols] = plain[t * inputs : (t + 1) * inputs]
                right[chan, at, cols] = turned[t * inputs : (t + 1) * inputs]

    def product(a, b):
        return lax.dot_general(a, b, (((1,), (1,)), ((), ())), preferred_element_type=jnp.float32)

    for tile in range(pairs_ref.shape[0]):
        rows = pl.ds(pl.multiple_of(pairs_ref[tile, 0] * TILE, TILE), TILE)
        cols = pl.ds(pl.multiple_of(pairs_ref[tile, 1] * TILE, TILE), TILE)
        for chan in range(chans):
            one = left[chan, rows, :]
            out_ref[0, chan, tile] = product(one, left[chan, cols, :]) * scale
            out_ref[1, chan, tile] = product(one, right[chan, cols, :]) * scale


def gram_call(got, tile_pairs, chans, total_spectra):
    rows, lanes = got.shape
    stations = 256
    depth = 8 * LANES
    vmem = pl.BlockSpec(memory_space=pltpu.VMEM)
    return pl.pallas_call(
        functools.partial(gram_kernel, 1.0 / total_spectra),
        out_shape=jax.ShapeDtypeStruct((2, chans, tile_pairs.shape[0], TILE, TILE), jnp.float32),
        in_specs=[pl.BlockSpec(memory_space=pltpu.SMEM), vmem],
        out_specs=vmem,
        scratch_shapes=[
            pltpu.VMEM((lanes // LANES, rows, LANES), jnp.float32),
            pltpu.VMEM((chans, stations, depth), jnp.bfloat16),
            pltpu.VMEM((chans, stations, depth), jnp.bfloat16),
        ],
        compiler_params=pltpu.CompilerParams(vmem_limit_bytes=VMEM_LIMIT),
        name="grams",
    )(tile_pairs, got)


def plans(frames, tap_count):
    ahead = tap_count - 1 - BACK

    def tap(out, j):
        frame = out - (tap_count - 1) + j
        if frame < 0:
            return (1, frame + ahead, False)
        if frame >= frames:
            return (2, frame - frames, False)
        return (0, frame, out >= frames)

    def plan(outs):
        return tuple(tuple(tap(out, j) for j in range(tap_count)) for out in outs)

    middle = list(range(tap_count - 1, tap_count - 1 + HALF))
    rest = list(range(tap_count - 1 + HALF, frames + BACK)) + list(range(BACK, tap_count - 1))
    return plan(middle), plan(rest)


def shards(volts, taps, tile_pairs):
    tap_count, fft_len = taps.shape
    frames = volts.shape[1] // fft_len
    peers = lax.axis_size("tm")
    ahead = tap_count - 1 - BACK
    earlier = lax.ppermute(
        volts[:, (frames - ahead) * fft_len :], "tm", [(i, i + 1) for i in range(peers - 1)]
    )
    later = lax.ppermute(volts[:, : BACK * fft_len], "tm", [(i, (i - 1) % peers) for i in range(peers)])
    table = jnp.asarray(second_step_table(fft_len))
    middle, rest = plans(frames, tap_count)
    keep = (lax.axis_index("tm") != peers - 1).astype(jnp.int32).reshape(1)
    spectra = spectra_call(middle, [volts], taps, table, keep, 0, None)
    spectra = spectra_call(rest, [volts, earlier, later], taps, table, keep, 1, spectra)
    devices = peers * lax.axis_size("stn")
    chans = fft_len // 2 // devices
    blocks = spectra.reshape(devices, 2 * chans, spectra.shape[1])
    got = lax.all_to_all(blocks, ("stn", "tm"), split_axis=0, concat_axis=0, tiled=True)
    return gram_call(got.reshape(spectra.shape), tile_pairs, chans, frames * peers)


def solution(mesh):
    return jax.shard_map(
        shards,
        mesh=mesh,
        in_specs=(P("stn", "tm"), P(), P()),
        out_specs=P(None, ("stn", "tm"), None, None, None),
        check_vma=False,
    )
```

time: 430 us -> 101 us (0.23)
  the two profiles are of different devices: /device:TPU:64 before, /device:TPU:1 now
where the time goes in v1:
time: 101 us; the launch traced here: 100 us
  waiting for transfers between devices  54.4 us (54%)
  Pallas kernels  21.6 us (21%)
  starting transfers between devices  19.7 us (20%)
  local copies, waits for them, and re-layouts  4.61 us (5%)
    all_to_all x1, waiting for transfers between devices, shards(): lax.all_to_all(blocks, ('stn', 'tm'), split_axis=0, concat_axis=0, tiled=...  54.4 us
    pallas_call x2, Pallas kernels, spectra_call(): pl.pallas_call(functools.partial(spectra_kernel, plan, fft_len), grid=(1,...  15.5 us
    all_to_all x1, starting transfers between devices, shards(): lax.all_to_all(blocks, ('stn', 'tm'), split_axis=0, concat_axis=0, tiled=...  10.7 us
    pallas_call x1, Pallas kernels, gram_call(): pl.pallas_call(functools.partial(gram_kernel, 1.0 / total_spectra), out_s...  6.09 us
    ppermute x1, starting transfers between devices, shards(): lax.ppermute(volts[:, :BACK * fft_len], 'tm', [(i, (i - 1) % peers) for i...  4.94 us
    ppermute x1, starting transfers between devices, shards(): lax.ppermute(volts[:, (frames - ahead) * fft_len:], 'tm', [(i, i + 1) for...  4.05 us
    unnamed x7, local copies, waits for them, and re-layouts  2.59 us
  transfers between devices with their start and end apart: 3, of which 1 were waited for; matrix products, arithmetic and copies ran while one was open for 1% of the time, Pallas kernels for 8%

profile of v1, /device:TPU:1, one launch (start us, length us, event | category | flops | bytes accessed | tf_op | source)
XLA Modules:
  0.0 100.3 jit_solution(7814622275713919516)
XLA Ops:
  0.0 1.0 %slice.6 = bf16[16,12288]{1,0:T(8,128)(2,1)S(1)} slice(bf16[16,65536]{1,0:T(8,128)(2,1)} %refs_0_.3), slice={[0:16], [53248:65536]} | slice | bytes 786432 | tf_op jit(solution)/shard_map/slice | solution.py:264
  1.0 4.1 %collective-permute-start = (bf16[16,12288]{1,0:T(8,128)(2,1)S(1)}, bf16[16,12288]{1,0:T(8,128)(2,1)S(1)}, u32[]{:S(2)}, u32[]{:S(2)}) collective-permute-start(bf16[16,12288]{1,0:T(8,128)(2,1)S(1)} %slice.6), channel_id=1, source_target_pairs={{0,1},{1,2},{2,3},{3,4},{4,5},{5,6},{6,7},{7,8},{8,9},{9,10},{10,1... | collective-permute-start | bytes 1179656 | tf_op jit(solution)/shard_map/ppermute | solution.py:263
  5.1 1.0 slice.7
  6.1 4.9 %collective-permute-start.1 = (bf16[16,10240]{1,0:T(8,128)(2,1)S(1)}, bf16[16,10240]{1,0:T(8,128)(2,1)S(1)}, u32[]{:S(2)}, u32[]{:S(2)}) collective-permute-start(bf16[16,10240]{1,0:T(8,128)(2,1)S(1)} %slice.7), channel_id=1, source_target_pairs={{0,15},{1,0},{2,1},{3,2},{4,3},{5,4},{6,5},{7,6},{8,7},{9,8},{10,9... | collective-permute-start | bytes 983048 | tf_op jit(solution)/shard_map/ppermute | solution.py:266
  11.0 0.0 copy-start
  11.0 1.6 %copy-done = bf16[16,65536]{1,0:T(8,128)(2,1)S(1)} copy-done((bf16[16,65536]{1,0:T(8,128)(2,1)S(1)}, bf16[16,65536]{1,0:T(8,128)(2,1)}, u32[]{:S(2)}) %copy-start) | copy-done | bytes 2097176
  12.6 0.0 copy-start.1
  12.6 0.9 copy-done.1
  13.5 7.7 %spectra0.1.refs_5_ = bf16[2048,512]{1,0:T(8,128)(2,1)} custom-call(s32[1]{0:T(128)} %bitcast.keep_ref, bf16[16,65536]{1,0:T(8,128)(2,1)S(1)} %copy-done, f32[12,2048]{1,0:T(8,128)S(1)} %copy-done.1, bf16[8,512,256]{2,1,0:T(8,128)(2,1)} %constant.8.clone.refs_2_.refs_4_), custom_call_target="tpu_custom_call" | custom-call | flops 1000000000 | bytes 6291456 | tf_op jit(solution)/shard_map/spectra0/pallas_call | solution.py:162
  21.2 0.0 collective-permute-done.1.refs_2_
  21.2 0.0 collective-permute-done.refs_1_
  21.2 7.8 %spectra1.1 = bf16[2048,512]{1,0:T(8,128)(2,1)} custom-call(s32[1]{0:T(128)} %bitcast.keep_ref, bf16[16,65536]{1,0:T(8,128)(2,1)S(1)} %copy-done, bf16[16,12288]{1,0:T(8,128)(2,1)S(1)} %collective-permute-done.refs_1_, bf16[16,10240]{1,0:T(8,128)(2,1)S(1)} %collective-permute-done.1.refs_2_, ...), custom_call_target="tpu_custom_call", output_to_operand_aliasing={{}: (6, {})} | custom-call | flops 1000000000 | bytes 6291456 | tf_op jit(solution)/shard_map/spectra1/pallas_call | solution.py:162
  29.0 0.0 copy-start.2
  29.0 10.7 %all-to-all-start = ((bf16[256,8,512]{2,1,0:T(8,128)(2,1)}), bf16[256,8,512]{2,1,0:T(8,128)(2,1)S(1)}, u32[]{:S(2)}, u32[]{:S(2)}) async-start(bf16[256,8,512]{2,1,0:T(8,128)(2,1)} %bitcast.1), calls=%async_computation | async-start | bytes 4194304 | tf_op jit(solution)/shard_map/all_to_all | solution.py:275
  39.7 0.0 copy-done.2
  39.7 0.1 copy.6.pairs_ref
  39.8 54.4 %all-to-all-done = bf16[256,8,512]{2,1,0:T(8,128)(2,1)S(1)} async-done(((bf16[256,8,512]{2,1,0:T(8,128)(2,1)}), bf16[256,8,512]{2,1,0:T(8,128)(2,1)S(1)}, u32[]{:S(2)}, u32[]{:S(2)}) %all-to-all-start) | async-done | bytes 2097184 | tf_op jit(solution)/shard_map/all_to_all | solution.py:275
  94.2 6.1 %grams.1 = f32[2,4,3,128,128]{4,3,2,1,0:T(8,128)} custom-call(s32[3,2]{1,0:T(4,128)S(1)} %copy.6.pairs_ref, bf16[2048,512]{1,0:T(8,128)(2,1)S(1)} %bitcast.3), custom_call_target="tpu_custom_call" | custom-call | tf_op jit(solution)/shard_map/grams/pallas_call | solution.py:224
Async XLA Ops:
  1.0 20.2 %collective-permute-start = (bf16[16,12288]{1,0:T(8,128)(2,1)S(1)}, bf16[16,12288]{1,0:T(8,128)(2,1)S(1)}, u32[]{:S(2)}, u32[]{:S(2)}) collective-permute-start(bf16[16,12288]{1,0:T(8,128)(2,1)S(1)} %slice.6), channel_id=1, source_target_pairs={{0,1},{1,2},{2,3},{3,4},{4,5},{5,6},{6,7},{7,8},{8,9},{9,10},{10,1... | collective-permute-start | bytes 1179656 | tf_op jit(solution)/shard_map/ppermute | solution.py:263
  6.1 15.1 %collective-permute-start.1 = (bf16[16,10240]{1,0:T(8,128)(2,1)S(1)}, bf16[16,10240]{1,0:T(8,128)(2,1)S(1)}, u32[]{:S(2)}, u32[]{:S(2)}) collective-permute-start(bf16[16,10240]{1,0:T(8,128)(2,1)S(1)} %slice.7), channel_id=1, source_target_pairs={{0,15},{1,0},{2,1},{3,2},{4,3},{5,4},{6,5},{7,6},{8,7},{9,8},{10,9... | collective-permute-start | bytes 983048 | tf_op jit(solution)/shard_map/ppermute | solution.py:266
  11.0 1.6 %copy-start = (bf16[16,65536]{1,0:T(8,128)(2,1)S(1)}, bf16[16,65536]{1,0:T(8,128)(2,1)}, u32[]{:S(2)}) copy-start(bf16[16,65536]{1,0:T(8,128)(2,1)} %refs_0_.3) | copy-start | bytes 6291460
  12.6 0.9 copy-start.1
  29.0 10.7 %copy-start.2 = (s32[3,2]{0,1:T(2,128)S(1)}, s32[3,2]{0,1:T(2,128)}, u32[]{:S(2)}) copy-start(s32[3,2]{0,1:T(2,128)} %param.6) | copy-start | bytes 76
  29.0 65.2 %all-to-all-start = ((bf16[256,8,512]{2,1,0:T(8,128)(2,1)}), bf16[256,8,512]{2,1,0:T(8,128)(2,1)S(1)}, u32[]{:S(2)}, u32[]{:S(2)}) async-start(bf16[256,8,512]{2,1,0:T(8,128)(2,1)} %bitcast.1), calls=%async_computation | async-start | bytes 4194304 | tf_op jit(solution)/shard_map/all_to_all | solution.py:275

commit v2 on v1

v2 whole, which is shorter than its diff:
```python
import functools
import math

import jax
import jax.numpy as jnp
import ml_dtypes
import numpy as np
from jax import lax
from jax.experimental import pallas as pl
from jax.experimental.pallas import tpu as pltpu
from jax.sharding import PartitionSpec as P

TILE = 128
LANES = 128
RADIX = 16
BACK = 5
BLOCK = 2
HALF = 16
Z_HIGH, PLANE, Z_LOW, Y_SIZE = 2, 8, 4, 4
Z_LOW_ORDER = (0, 2, 1, 3)
VMEM_LIMIT = 48 * 1024 * 1024


def device_order():
    order = []
    for plane in range(PLANE):
        for y in range(Y_SIZE):
            for low in Z_LOW_ORDER:
                for high in range(Z_HIGH):
                    order.append(((high * PLANE + plane) * Z_LOW + low) * Y_SIZE + y)
    return order


def second_step_table(fft_len):
    length = fft_len // RADIX
    quarter = length // 2
    place = np.arange(length, dtype=np.int64)
    out = np.zeros((RADIX // 2, 2 * length, 2 * length), np.float64)
    column = np.array([dev // Y_SIZE for dev in device_order() if dev % Y_SIZE == 0], np.int64)

    def rows(kappa):
        chan = kappa + RADIX * column
        angle = 2.0 * np.pi * ((chan[:, None] * place[None, :]) % fft_len) / fft_len
        return np.cos(angle), np.sin(angle)

    for pair in range(RADIX // 2):
        for slot in range(2):
            if pair == 0:
                kappa = 0 if slot == 0 else RADIX // 2
            else:
                kappa = pair if slot == 0 else RADIX - pair
            cos, sin = rows(kappa)
            first = slot * length
            if pair == 0:
                cols = slice(slot * length, (slot + 1) * length)
                out[pair, first : first + quarter, cols] = cos
                out[pair, first + quarter : first + length, cols] = -sin
            else:
                sign = 1.0 if slot == 0 else -1.0
                out[pair, first : first + quarter, :length] = cos
                out[pair, first : first + quarter, length:] = -sign * sin
                out[pair, first + quarter : first + length, :length] = -sin
                out[pair, first + quarter : first + length, length:] = -sign * cos
    out = (out / math.sqrt(fft_len)).astype(np.float32)
    high = out.astype(ml_dtypes.bfloat16)
    low = (out - high.astype(np.float32)).astype(ml_dtypes.bfloat16)
    return np.concatenate([high, low], axis=1)


def first_step(x):
    c1, c2, c3 = (math.cos(math.pi * j / 8) for j in (1, 2, 3))
    a = [x[n] + x[n + 8] for n in range(8)]
    b = [x[n] - x[n + 8] for n in range(8)]
    d = [None] + [b[n] - b[8 - n] for n in (1, 2, 3)]
    s = [None] + [b[n] + b[8 - n] for n in (1, 2, 3)]
    u, v = b[0] + c2 * d[2], b[0] - c2 * d[2]
    p, q = c1 * d[1] + c3 * d[3], c3 * d[1] - c1 * d[3]
    g, h = b[4] + c2 * s[2], b[4] - c2 * s[2]
    m, n = c3 * s[1] + c1 * s[3], c1 * s[1] - c3 * s[3]
    e = [a[n_] + a[n_ + 4] for n_ in range(4)]
    f = [a[n_] - a[n_ + 4] for n_ in range(4)]
    w, z = c2 * (f[1] - f[3]), c2 * (f[1] + f[3])
    even, odd = e[0] + e[2], e[1] + e[3]
    return [
        (even + odd, even - odd),
        (u + p, g + m),
        (f[0] + w, f[2] + z),
        (v + q, n - h),
        (e[0] - e[2], e[1] - e[3]),
        (v - q, h + n),
        (f[0] - w, z - f[2]),
        (u - p, m - g),
    ]


def filter_outputs(plan, fft_len, keep, sources, taps_ref, filt, blocks=None):
    rows = sources[0].shape[0]
    tap_count = taps_ref.shape[0]

    @pl.loop(0, RADIX)
    def _(col):
        base = pl.multiple_of(col * LANES, LANES)
        weights = [
            jnp.broadcast_to(taps_ref[pl.ds(j, 1), pl.ds(base, LANES)], (rows, LANES)) for j in range(tap_count)
        ]
        for block in range(0, len(plan), BLOCK):
            held = {}
            for out in range(block, min(block + BLOCK, len(plan))):
                sums = {False: None, True: None}
                for j, (src, frame, wiped) in enumerate(plan[out]):
                    if (src, frame) not in held:
                        lane = pl.multiple_of(frame * fft_len + base, LANES)
                        held[src, frame] = sources[src][:, pl.ds(lane, LANES)].astype(jnp.float32)
                    term = held[src, frame] * weights[j]
                    sums[wiped] = term if sums[wiped] is None else sums[wiped] + term
                total = sums[False]
                if sums[True] is not None:
                    total = total + jnp.where(keep, sums[True], 0.0)
                filt[pl.ds(out * rows, rows), pl.ds(base, LANES)] = total


def first_steps(filt, rows, first, count, high, low, offset):
    @pl.loop(0, count)
    def _(out):
        at = pl.ds(pl.multiple_of((out + first) * rows, rows), rows)
        to = pl.ds(pl.multiple_of(out * rows + offset, rows), rows)
        parts = first_step([filt[at, n * LANES : (n + 1) * LANES] for n in range(RADIX)])
        for pair, halves in enumerate(parts):
            for k, value in enumerate(halves):
                top = value.astype(jnp.bfloat16)
                high[pair, to, k * LANES : (k + 1) * LANES] = top
                low[pair, to, k * LANES : (k + 1) * LANES] = (value - top.astype(jnp.float32)).astype(jnp.bfloat16)


def second_steps(table, high, low, turned, out_ref):
    quarter = PLANE * Z_HIGH * Z_LOW
    per_dev = 4
    z_size = Z_HIGH * Z_LOW
    block = 2 * per_dev

    def product(left, right):
        return lax.dot_general(left, right, (((1,), (1,)), ((), ())), preferred_element_type=jnp.float32)

    size = 2 * LANES
    for pair in range(RADIX // 2):
        table_high, table_low = table[pair, :size], table[pair, size:]
        result = (
            product(table_high, low[pair]) + product(table_low, high[pair])
        ) + product(table_high, high[pair])
        for slot in range(2):
            kappa = (pair, RADIX - pair)[slot] if pair else (0, RADIX // 2)[slot]
            for part in range(2):
                for plane in range(PLANE):
                    first = slot * LANES + part * quarter + plane * z_size
                    row = (plane * Y_SIZE + kappa // per_dev) * z_size * block + (kappa % per_dev) * 2 + part
                    for lane in range(result.shape[1] // LANES):
                        turned[lane, pl.ds(row, z_size, stride=block), :] = result[
                            first : first + z_size, lane * LANES : (lane + 1) * LANES
                        ]
    for lane in range(turned.shape[0]):
        out_ref[:, lane * LANES : (lane + 1) * LANES] = turned[lane].astype(jnp.bfloat16)


def middle_kernel(plan, fft_len, volts, taps, table_hbm, out_ref, more_high, more_low,
                  table, filt, high, low, turned, sems):
    rows = volts.shape[0]
    copy = pltpu.make_async_copy(table_hbm, table, sems.at[0])
    copy.start()
    filter_outputs(plan, fft_len, None, [volts], taps, filt)
    first_steps(filt, rows, 0, HALF, high, low, 0)
    first_steps(filt, rows, HALF, len(plan) - HALF, more_high, more_low, 0)
    copy.wait()
    second_steps(table, high, low, turned, out_ref)


def edge_kernel(plan, fft_len, keep_ref, volts, taps, table_hbm, earlier, later, more_high, more_low, _,
                out_ref, table, filt, high, low, turned, sems):
    rows = volts.shape[0]
    copies = [
        pltpu.make_async_copy(more_high, high.at[:, pl.ds(0, more_high.shape[1])], sems.at[0]),
        pltpu.make_async_copy(more_low, low.at[:, pl.ds(0, more_low.shape[1])], sems.at[1]),
        pltpu.make_async_copy(table_hbm, table, sems.at[2]),
    ]
    for copy in copies:
        copy.start()
    filter_outputs(plan, fft_len, keep_ref[0] != 0, [volts, earlier, later], taps, filt)
    first_steps(filt, rows, 0, len(plan), high, low, more_high.shape[1])
    for copy in copies:
        copy.wait()
    second_steps(table, high, low, turned, out_ref)


def spectra_scratch(volts, taps, table, outputs, copies):
    rows, fft_len = volts.shape[0], taps.shape[1]
    cols = HALF * rows
    return [
        pltpu.VMEM(table.shape, table.dtype),
        pltpu.VMEM((outputs * rows, fft_len), jnp.float32),
        pltpu.VMEM((RADIX // 2, cols, 2 * LANES), jnp.bfloat16),
        pltpu.VMEM((RADIX // 2, cols, 2 * LANES), jnp.bfloat16),
        pltpu.VMEM((cols // LANES, fft_len, LANES), jnp.float32),
        pltpu.SemaphoreType.DMA((copies,)),
    ]


def middle_call(plan, volts, taps, table):
    rows, fft_len = volts.shape[0], taps.shape[1]
    cols = HALF * rows
    more = jax.ShapeDtypeStruct((RADIX // 2, (len(plan) - HALF) * rows, 2 * LANES), jnp.bfloat16)
    whole = pl.BlockSpec(more.shape, lambda i: (0, 0, 0))
    vmem = pl.BlockSpec(memory_space=pltpu.VMEM)
    return pl.pallas_call(
        functools.partial(middle_kernel, plan, fft_len),
        grid=(1,),
        out_shape=(pltpu.HBM((fft_len, 2 * cols), jnp.bfloat16), more, more),
        in_specs=[vmem, vmem, pl.BlockSpec(memory_space=pl.ANY)],
        out_specs=(pl.BlockSpec((fft_len, cols), lambda i: (0, 0)), whole, whole),
        scratch_shapes=spectra_scratch(volts, taps, table, len(plan), 1),
        compiler_params=pltpu.CompilerParams(vmem_limit_bytes=VMEM_LIMIT),
        cost_estimate=pl.CostEstimate(flops=10**9, bytes_accessed=8 * 2**20, transcendentals=0),
        name="middle",
    )(volts, taps, table)


def edge_call(plan, keep, volts, taps, table, earlier, later, more_high, more_low, spectra):
    rows, fft_len = volts.shape[0], taps.shape[1]
    cols = HALF * rows
    hbm = pl.BlockSpec(memory_space=pl.ANY)
    vmem = pl.BlockSpec(memory_space=pltpu.VMEM)
    return pl.pallas_call(
        functools.partial(edge_kernel, plan, fft_len),
        grid=(1,),
        out_shape=pltpu.HBM(spectra.shape, spectra.dtype),
        in_specs=[pl.BlockSpec(memory_space=pltpu.SMEM), vmem, vmem, hbm, vmem, vmem, hbm, hbm, hbm],
        out_specs=pl.BlockSpec((fft_len, cols), lambda i: (0, 1)),
        scratch_shapes=spectra_scratch(volts, taps, table, len(plan), 3),
        input_output_aliases={8: 0},
        compiler_params=pltpu.CompilerParams(vmem_limit_bytes=VMEM_LIMIT),
        cost_estimate=pl.CostEstimate(flops=10**9, bytes_accessed=8 * 2**20, transcendentals=0),
        name="edge",
    )(keep, volts, taps, table, earlier, later, more_high, more_low, spectra)


def ends_kernel(volts, last_ref, first_ref, sems):
    size = last_ref.shape[1]
    copies = [
        pltpu.make_async_copy(volts.at[:, pl.ds(volts.shape[1] - size, size)], last_ref, sems.at[0]),
        pltpu.make_async_copy(volts.at[:, pl.ds(0, first_ref.shape[1])], first_ref, sems.at[1]),
    ]
    for copy in copies:
        copy.start()
    for copy in copies:
        copy.wait()


def ends_call(volts, last, first):
    vmem = pl.BlockSpec(memory_space=pltpu.VMEM)
    rows = volts.shape[0]
    return pl.pallas_call(
        ends_kernel,
        out_shape=(jax.ShapeDtypeStruct((rows, last), volts.dtype), jax.ShapeDtypeStruct((rows, first), volts.dtype)),
        in_specs=[pl.BlockSpec(memory_space=pl.ANY)],
        out_specs=(vmem, vmem),
        scratch_shapes=[pltpu.SemaphoreType.DMA((2,))],
        name="ends",
    )(volts)


def gram_kernel(scale, pairs_ref, got_ref, out_ref, wide, both, tiles):
    groups = wide.shape[0]
    per_src = 8
    times = Y_SIZE * Z_LOW
    inputs = LANES // 8
    pitch = 3 * per_src
    chan = pl.program_id(0)

    @pl.when(chan == 0)
    def _():
        @pl.loop(0, got_ref.shape[0] // (2 * per_src), unroll=8)
        def _(two):
            from_rows = pl.ds(pl.multiple_of(two * 2 * per_src, 2 * per_src), 2 * per_src)
            to_rows = pl.ds(pl.multiple_of(two * pitch, per_src), 2 * per_src)
            for group in range(groups):
                wide[group, to_rows] = got_ref[from_rows, group * LANES : (group + 1) * LANES].astype(jnp.float32)

    stations = Z_HIGH * PLANE * inputs

    @pl.loop(0, Z_HIGH * PLANE, unroll=16)
    def _(stn):
        at = pl.ds(pl.multiple_of(stn * inputs, inputs), inputs)
        turned_at = pl.ds(pl.multiple_of(stations + stn * inputs, inputs), inputs)
        first = (stn % PLANE) * times * pitch + (stn // PLANE) * per_src + chan * 2
        parts = [
            [wide[group, pl.ds(first + part, times, stride=pitch), :] for group in range(groups)] for part in range(2)
        ]
        plain = jnp.concatenate(parts[0] + parts[1], 0).astype(jnp.bfloat16).T
        turned = jnp.concatenate([-v for v in parts[1]] + parts[0], 0).astype(jnp.bfloat16).T
        for t in range(LANES // inputs):
            cols = slice(t * LANES, (t + 1) * LANES)
            both[at, cols] = plain[t * inputs : (t + 1) * inputs]
            both[turned_at, cols] = turned[t * inputs : (t + 1) * inputs]

    sums = lax.dot_general(
        both[:stations], both[...], (((1,), (1,)), ((), ())), preferred_element_type=jnp.float32
    )
    for first in range(2):
        for second in range(2):
            for part in range(2):
                col = part * stations + second * TILE
                tiles[first, second, part] = sums[first * TILE : (first + 1) * TILE, col : col + TILE] * scale
    for tile in range(pairs_ref.shape[0]):
        for part in range(2):
            out_ref[part, 0, tile] = tiles[pairs_ref[tile, 0], pairs_ref[tile, 1], part]


def gram_call(got, tile_pairs, chans, total_spectra):
    rows, lanes = got.shape
    stations = 2 * TILE
    depth = 8 * LANES
    tiles = tile_pairs.shape[0]
    return pl.pallas_call(
        functools.partial(gram_kernel, 1.0 / total_spectra),
        grid=(chans,),
        out_shape=jax.ShapeDtypeStruct((2, chans, tiles, TILE, TILE), jnp.float32),
        in_specs=[pl.BlockSpec(memory_space=pltpu.SMEM), pl.BlockSpec(memory_space=pltpu.VMEM)],
        out_specs=pl.BlockSpec((2, 1, tiles, TILE, TILE), lambda i: (0, i, 0, 0, 0)),
        scratch_shapes=[
            pltpu.VMEM((lanes // LANES, rows // 2 * 3, LANES), jnp.float32),
            pltpu.VMEM((2 * stations, depth), jnp.bfloat16),
            pltpu.VMEM((2, 2, 2, TILE, TILE), jnp.float32),
        ],
        compiler_params=pltpu.CompilerParams(vmem_limit_bytes=VMEM_LIMIT),
        name="grams",
    )(tile_pairs, got)


def plans(frames, tap_count):
    ahead = tap_count - 1 - BACK

    def tap(out, j):
        frame = out - (tap_count - 1) + j
        if frame < 0:
            return (1, frame + ahead, False)
        if frame >= frames:
            return (2, frame - frames, False)
        return (0, frame, out >= frames)

    def plan(outs):
        return tuple(tuple(tap(out, j) for j in range(tap_count)) for out in outs)

    middle = list(range(tap_count - 1, frames))
    edges = list(range(BACK, tap_count - 1)) + list(range(frames, frames + BACK))
    return plan(middle), plan(edges)


def shards(volts, taps, tile_pairs):
    tap_count, fft_len = taps.shape
    frames = volts.shape[1] // fft_len
    peers = lax.axis_size("tm")
    last, first = ends_call(volts, (tap_count - 1 - BACK) * fft_len, BACK * fft_len)
    earlier = lax.ppermute(last, "tm", [(i, i + 1) for i in range(peers - 1)])
    later = lax.ppermute(first, "tm", [(i, (i - 1) % peers) for i in range(peers)])
    table = jnp.asarray(second_step_table(fft_len))
    middle, edges = plans(frames, tap_count)
    keep = (lax.axis_index("tm") != peers - 1).astype(jnp.int32).reshape(1)
    spectra, more_high, more_low = middle_call(middle, volts, taps, table)
    spectra = edge_call(edges, keep, volts, taps, table, earlier, later, more_high, more_low, spectra)
    order = device_order()
    chans = fft_len // 2 // len(order)
    blocks = spectra.reshape(len(order), 2 * chans, spectra.shape[1])
    got = lax.all_to_all(
        blocks, ("stn", "tm"), split_axis=0, concat_axis=0, tiled=True, axis_index_groups=[order]
    )
    return gram_call(got.reshape(spectra.shape), tile_pairs, chans, frames * peers)


def solution(mesh):
    return jax.shard_map(
        shards,
        mesh=mesh,
        in_specs=(P("stn", "tm"), P(), P()),
        out_specs=P(None, ("stn", "tm"), None, None, None),
        check_vma=False,
    )
```

time: 101 us -> 93.8 us (0.929)
  Pallas kernels: 21.6 us -> 17.2 us
  local copies, waits for them, and re-layouts: 4.61 us -> 2.6 us
  waiting for transfers between devices: 54.4 us -> 52.4 us
  starting transfers between devices: 19.7 us -> 21.3 us
    pallas_call x3 -> x4, Pallas kernels: 21.6 us -> 17.2 us  [the longest x1 5.8 us: middle_call(): pl.pallas_call(functools.partial(middle_kernel, plan, fft_len), grid=(1,)...]
    slice x2 -> x0, local copies, waits for them, and re-layouts: 2.02 us -> none  [the longest x1 1.02 us: shards(): volts[:, (frames - ahead) * fft_len:]]
    all_to_all x1, waiting for transfers between devices: 54.4 us -> 52.4 us  [shards(): lax.all_to_all(blocks, ('stn', 'tm'), split_axis=0, concat_axis=0, tiled=...]
    all_to_all x1, starting transfers between devices: 10.7 us -> 12.3 us  [shards(): lax.all_to_all(blocks, ('stn', 'tm'), split_axis=0, concat_axis=0, tiled=...]
    unnamed x7 -> x9, local copies, waits for them, and re-layouts: 2.59 us -> 2.6 us
  transfers between devices with their start and end apart: 3 -> 3, of which waited for: 1 -> 1; matrix products, arithmetic and copies ran while one was open for 1% -> 0% of each run, Pallas kernels for 8% -> 6%
where the time goes in v2:
time: 93.8 us; the launch traced here: 93.6 us
  waiting for transfers between devices  52.4 us (56%)
  starting transfers between devices  21.3 us (23%)
  Pallas kernels  17.2 us (18%)
  local copies, waits for them, and re-layouts  2.6 us (3%)
    all_to_all x1, waiting for transfers between devices, shards(): lax.all_to_all(blocks, ('stn', 'tm'), split_axis=0, concat_axis=0, tiled=...  52.4 us
    all_to_all x1, starting transfers between devices, shards(): lax.all_to_all(blocks, ('stn', 'tm'), split_axis=0, concat_axis=0, tiled=...  12.3 us
    pallas_call x1, Pallas kernels, middle_call(): pl.pallas_call(functools.partial(middle_kernel, plan, fft_len), grid=(1,)...  5.8 us
    ppermute x1, starting transfers between devices, shards(): lax.ppermute(first, 'tm', [(i, (i - 1) % peers) for i in range(peers)])  4.94 us
    pallas_call x1, Pallas kernels, gram_call(): pl.pallas_call(functools.partial(gram_kernel, 1.0 / total_spectra), grid=...  4.9 us
    pallas_call x1, Pallas kernels, edge_call(): pl.pallas_call(functools.partial(edge_kernel, plan, fft_len), grid=(1,),...  4.4 us
    ppermute x1, starting transfers between devices, shards(): earlier = lax.ppermute(last, 'tm', [(i, i + 1) for i in range(peers - 1)])  4.05 us
    unnamed x9, local copies, waits for them, and re-layouts  2.6 us
  transfers between devices with their start and end apart: 3, of which 1 were waited for; matrix products, arithmetic and copies ran while one was open for 0% of the time, Pallas kernels for 6%

profile of v2, /device:TPU:1, one launch (start us, length us, event | category | flops | bytes accessed | tf_op | source)
XLA Modules:
  0.0 93.6 jit_solution(10328680644825809218)
XLA Ops:
  0.0 0.0 copy-start
  0.0 2.1 %ends.1 = (bf16[16,12288]{1,0:T(8,128)(2,1)}, bf16[16,10240]{1,0:T(8,128)(2,1)}) custom-call(bf16[16,65536]{1,0:T(8,128)(2,1)} %volts.5), custom_call_target="tpu_custom_call" | custom-call | tf_op jit(solution)/shard_map/ends/pallas_call | solution.py:259
  2.1 4.1 %collective-permute-start = (bf16[16,12288]{1,0:T(8,128)(2,1)}, bf16[16,12288]{1,0:T(8,128)(2,1)S(1)}, u32[]{:S(2)}, u32[]{:S(2)}) collective-permute-start(bf16[16,12288]{1,0:T(8,128)(2,1)} %get-tuple-element.10), channel_id=1, source_target_pairs={{0,1},{1,2},{2,3},{3,4},{4,5},{5,6},{6,7},{7,8},{8,9},{9,10},{10,1... | collective-permute-start | bytes 1179656 | tf_op jit(solution)/shard_map/ppermute | solution.py:361
  6.2 4.9 %collective-permute-start.1 = (bf16[16,10240]{1,0:T(8,128)(2,1)}, bf16[16,10240]{1,0:T(8,128)(2,1)S(1)}, u32[]{:S(2)}, u32[]{:S(2)}) collective-permute-start(bf16[16,10240]{1,0:T(8,128)(2,1)} %get-tuple-element.11), channel_id=1, source_target_pairs={{0,15},{1,0},{2,1},{3,2},{4,3},{5,4},{6,5},{7,6},{8,7},{9,8},{10,9... | collective-permute-start | bytes 983048 | tf_op jit(solution)/shard_map/ppermute | solution.py:362
  11.1 0.0 copy-done
  11.1 0.0 copy-start.1
  11.1 1.6 %copy-done.1 = bf16[8,512,256]{2,1,0:T(8,128)(2,1)S(1)} copy-done((bf16[8,512,256]{2,1,0:T(8,128)(2,1)S(1)}, bf16[8,512,256]{2,1,0:T(8,128)(2,1)}, u32[]{:S(2)}) %copy-start.1) | copy-done | bytes 2097176
  12.7 0.0 copy-start.2
  12.7 0.9 copy-done.2
  13.6 5.8 %middle.1 = (bf16[2048,512]{1,0:T(8,128)(2,1)}, bf16[8,80,256]{2,1,0:T(8,128)(2,1)S(1)}, bf16[8,80,256]{2,1,0:T(8,128)(2,1)S(1)}) custom-call(bf16[16,65536]{1,0:T(8,128)(2,1)S(1)} %copy-done, f32[12,2048]{1,0:T(8,128)S(1)} %copy-done.2, bf16[8,512,256]{2,1,0:T(8,128)(2,1)S(1)} %copy-done.1), custom_call_target="tpu_custom_call" | custom-call | flops 1000000000 | bytes 8388608 | tf_op jit(solution)/shard_map/middle/pallas_call | solution.py:212
  19.4 0.0 collective-permute-done.1.later
  19.4 0.0 collective-permute-done.earlier
  19.4 4.4 %edge.1 = bf16[2048,512]{1,0:T(8,128)(2,1)} custom-call(s32[1]{0:T(128)} %bitcast.keep_ref, bf16[16,65536]{1,0:T(8,128)(2,1)S(1)} %copy-done, f32[12,2048]{1,0:T(8,128)S(1)} %copy-done.2, bf16[8,512,256]{2,1,0:T(8,128)(2,1)S(1)} %copy-done.1, bf16[16,12288]{1,0:T(8,128)(2,1)S(1)} %collective-permute-done.earlier, ...), custom_call_target="tpu_custom_call", output_to_operand_aliasing={{}: (8, {})} | custom-call | flops 1000000000 | bytes 8388608 | tf_op jit(solution)/shard_map/edge/pallas_call | solution.py:230
  23.9 0.0 copy-start.3
  23.9 12.3 %all-to-all-start = ((bf16[256,8,512]{2,1,0:T(8,128)(2,1)}), bf16[256,8,512]{2,1,0:T(8,128)(2,1)S(1)}, u32[]{:S(2)}, u32[]{:S(2)}) async-start(bf16[256,8,512]{2,1,0:T(8,128)(2,1)} %bitcast.4), calls=%async_computation | async-start | bytes 4194304 | tf_op jit(solution)/shard_map/all_to_all | solution.py:371
  36.2 0.0 copy-done.3
  36.2 0.1 copy.6.pairs_ref
  36.3 52.4 %all-to-all-done = bf16[256,8,512]{2,1,0:T(8,128)(2,1)S(1)} async-done(((bf16[256,8,512]{2,1,0:T(8,128)(2,1)}), bf16[256,8,512]{2,1,0:T(8,128)(2,1)S(1)}, u32[]{:S(2)}, u32[]{:S(2)}) %all-to-all-start) | async-done | bytes 2097184 | tf_op jit(solution)/shard_map/all_to_all | solution.py:371
  88.7 4.9 %grams.1 = f32[2,4,3,128,128]{4,3,2,1,0:T(8,128)} custom-call(s32[3,2]{1,0:T(4,128)S(1)} %copy.6.pairs_ref, bf16[2048,512]{1,0:T(8,128)(2,1)S(1)} %bitcast.3), custom_call_target="tpu_custom_call" | custom-call | tf_op jit(solution)/shard_map/grams/pallas_call | solution.py:321
Async XLA Ops:
  0.0 11.1 %copy-start = (bf16[16,65536]{1,0:T(8,128)(2,1)S(1)}, bf16[16,65536]{1,0:T(8,128)(2,1)}, u32[]{:S(2)}) copy-start(bf16[16,65536]{1,0:T(8,128)(2,1)} %volts.5) | copy-start | bytes 6291460
  2.1 17.3 %collective-permute-start = (bf16[16,12288]{1,0:T(8,128)(2,1)}, bf16[16,12288]{1,0:T(8,128)(2,1)S(1)}, u32[]{:S(2)}, u32[]{:S(2)}) collective-permute-start(bf16[16,12288]{1,0:T(8,128)(2,1)} %get-tuple-element.10), channel_id=1, source_target_pairs={{0,1},{1,2},{2,3},{3,4},{4,5},{5,6},{6,7},{7,8},{8,9},{9,10},{10,1... | collective-permute-start | bytes 1179656 | tf_op jit(solution)/shard_map/ppermute | solution.py:361
  6.2 13.3 %collective-permute-start.1 = (bf16[16,10240]{1,0:T(8,128)(2,1)}, bf16[16,10240]{1,0:T(8,128)(2,1)S(1)}, u32[]{:S(2)}, u32[]{:S(2)}) collective-permute-start(bf16[16,10240]{1,0:T(8,128)(2,1)} %get-tuple-element.11), channel_id=1, source_target_pairs={{0,15},{1,0},{2,1},{3,2},{4,3},{5,4},{6,5},{7,6},{8,7},{9,8},{10,9... | collective-permute-start | bytes 983048 | tf_op jit(solution)/shard_map/ppermute | solution.py:362
  11.1 1.6 %copy-start.1 = (bf16[8,512,256]{2,1,0:T(8,128)(2,1)S(1)}, bf16[8,512,256]{2,1,0:T(8,128)(2,1)}, u32[]{:S(2)}) copy-start(bf16[8,512,256]{2,1,0:T(8,128)(2,1)} %constant.8.clone.table_hbm) | copy-start | bytes 6291460
  12.7 0.9 copy-start.2
  23.9 12.3 %copy-start.3 = (s32[3,2]{0,1:T(2,128)S(1)}, s32[3,2]{0,1:T(2,128)}, u32[]{:S(2)}) copy-start(s32[3,2]{0,1:T(2,128)} %param.6) | copy-start | bytes 76
  23.9 64.8 %all-to-all-start = ((bf16[256,8,512]{2,1,0:T(8,128)(2,1)}), bf16[256,8,512]{2,1,0:T(8,128)(2,1)S(1)}, u32[]{:S(2)}, u32[]{:S(2)}) async-start(bf16[256,8,512]{2,1,0:T(8,128)(2,1)} %bitcast.4), calls=%async_computation | async-start | bytes 4194304 | tf_op jit(solution)/shard_map/all_to_all | solution.py:371

commit v3 on v2

v3 whole, which is shorter than its diff:
```python
import functools
import math

import jax
import jax.numpy as jnp
import ml_dtypes
import numpy as np
from jax import lax
from jax.experimental import pallas as pl
from jax.experimental.pallas import tpu as pltpu
from jax.sharding import PartitionSpec as P

TILE = 128
LANES = 128
RADIX = 16
BACK = 5
BLOCK = 2
HALF = 16
Z_HIGH, PLANE, Z_LOW, Y_SIZE = 2, 8, 4, 4
Z_LOW_ORDER = (0, 2, 1, 3)
VMEM_LIMIT = 48 * 1024 * 1024


def device_order():
    order = []
    for plane in range(PLANE):
        for y in range(Y_SIZE):
            for low in Z_LOW_ORDER:
                for high in range(Z_HIGH):
                    order.append(((high * PLANE + plane) * Z_LOW + low) * Y_SIZE + y)
    return order


def second_step_table(fft_len):
    length = fft_len // RADIX
    quarter = length // 2
    place = np.arange(length, dtype=np.int64)
    out = np.zeros((RADIX // 2, 2 * length, 2 * length), np.float64)
    column = np.array([dev // Y_SIZE for dev in device_order() if dev % Y_SIZE == 0], np.int64)

    def rows(kappa):
        chan = kappa + RADIX * column
        angle = 2.0 * np.pi * ((chan[:, None] * place[None, :]) % fft_len) / fft_len
        return np.cos(angle), np.sin(angle)

    for pair in range(RADIX // 2):
        for slot in range(2):
            if pair == 0:
                kappa = 0 if slot == 0 else RADIX // 2
            else:
                kappa = pair if slot == 0 else RADIX - pair
            cos, sin = rows(kappa)
            first = slot * length
            if pair == 0:
                cols = slice(slot * length, (slot + 1) * length)
                out[pair, first : first + quarter, cols] = cos
                out[pair, first + quarter : first + length, cols] = -sin
            else:
                sign = 1.0 if slot == 0 else -1.0
                out[pair, first : first + quarter, :length] = cos
                out[pair, first : first + quarter, length:] = -sign * sin
                out[pair, first + quarter : first + length, :length] = -sin
                out[pair, first + quarter : first + length, length:] = -sign * cos
    out = (out / math.sqrt(fft_len)).astype(np.float32)
    high = out.astype(ml_dtypes.bfloat16)
    low = (out - high.astype(np.float32)).astype(ml_dtypes.bfloat16)
    return np.concatenate([high, low], axis=1)


def first_step(x):
    c1, c2, c3 = (math.cos(math.pi * j / 8) for j in (1, 2, 3))
    a = [x[n] + x[n + 8] for n in range(8)]
    b = [x[n] - x[n + 8] for n in range(8)]
    d = [None] + [b[n] - b[8 - n] for n in (1, 2, 3)]
    s = [None] + [b[n] + b[8 - n] for n in (1, 2, 3)]
    u, v = b[0] + c2 * d[2], b[0] - c2 * d[2]
    p, q = c1 * d[1] + c3 * d[3], c3 * d[1] - c1 * d[3]
    g, h = b[4] + c2 * s[2], b[4] - c2 * s[2]
    m, n = c3 * s[1] + c1 * s[3], c1 * s[1] - c3 * s[3]
    e = [a[n_] + a[n_ + 4] for n_ in range(4)]
    f = [a[n_] - a[n_ + 4] for n_ in range(4)]
    w, z = c2 * (f[1] - f[3]), c2 * (f[1] + f[3])
    even, odd = e[0] + e[2], e[1] + e[3]
    return [
        (even + odd, even - odd),
        (u + p, g + m),
        (f[0] + w, f[2] + z),
        (v + q, n - h),
        (e[0] - e[2], e[1] - e[3]),
        (v - q, h + n),
        (f[0] - w, z - f[2]),
        (u - p, m - g),
    ]


def filter_outputs(plan, fft_len, keep, sources, taps_ref, base_ref, out_ref, start):
    rows = sources[0].shape[0]

    @pl.loop(0, RADIX)
    def _(col):
        base = pl.multiple_of(col * LANES, LANES)
        lanes = pl.ds(base, LANES)
        weights = [jnp.broadcast_to(taps_ref[pl.ds(j, 1), lanes], (rows, LANES)) for j in range(taps_ref.shape[0])]
        for block in range(0, len(plan), BLOCK):
            held = {}
            for out in range(block, min(block + BLOCK, len(plan))):
                at = pl.ds((start + out) * rows, rows)
                sums = {False: None if base_ref is None else base_ref[at, lanes], True: None}
                for j, src, frame, wiped in plan[out]:
                    if (src, frame) not in held:
                        lane = pl.multiple_of(frame * fft_len + base, LANES)
                        held[src, frame] = sources[src][:, pl.ds(lane, LANES)].astype(jnp.float32)
                    term = held[src, frame] * weights[j]
                    sums[wiped] = term if sums[wiped] is None else sums[wiped] + term
                total = sums[False]
                if sums[True] is not None:
                    wiped_sum = jnp.where(keep, sums[True], 0.0)
                    total = wiped_sum if total is None else total + wiped_sum
                out_ref[at, lanes] = total


def first_steps(filt, rows, first, count, high, low, offset):
    @pl.loop(0, count)
    def _(out):
        at = pl.ds(pl.multiple_of((out + first) * rows, rows), rows)
        to = pl.ds(pl.multiple_of(out * rows + offset, rows), rows)
        parts = first_step([filt[at, n * LANES : (n + 1) * LANES] for n in range(RADIX)])
        for pair, halves in enumerate(parts):
            for k, value in enumerate(halves):
                top = value.astype(jnp.bfloat16)
                high[pair, to, k * LANES : (k + 1) * LANES] = top
                low[pair, to, k * LANES : (k + 1) * LANES] = (value - top.astype(jnp.float32)).astype(jnp.bfloat16)


def second_steps(table, high, low, turned, ready, out_ref, half, sems):
    quarter = PLANE * Z_HIGH * Z_LOW
    per_dev = 4
    z_size = Z_HIGH * Z_LOW
    block = 2 * per_dev
    share = z_size * block
    cols = ready.shape[1]

    def product(left, right):
        return lax.dot_general(left, right, (((1,), (1,)), ((), ())), preferred_element_type=jnp.float32)

    def send(first_y, count, sem):
        copies = []
        for plane in range(PLANE):
            at = pl.ds((plane * Y_SIZE + first_y) * share, count * share)
            for lane in range(cols // LANES):
                ready[at, lane * LANES : (lane + 1) * LANES] = turned[lane, at].astype(jnp.bfloat16)
            copies.append(
                pltpu.make_async_copy(ready.at[at], out_ref.at[at, pl.ds(half * cols, cols)], sems.at[sem + plane])
            )
            copies[-1].start()
        return copies

    size = 2 * LANES
    copies = []
    for pair in range(RADIX // 2):
        table_high, table_low = table[pair, :size], table[pair, size:]
        result = (
            product(table_high, low[pair]) + product(table_low, high[pair])
        ) + product(table_high, high[pair])
        for slot in range(2):
            kappa = (pair, RADIX - pair)[slot] if pair else (0, RADIX // 2)[slot]
            for part in range(2):
                for plane in range(PLANE):
                    first = slot * LANES + part * quarter + plane * z_size
                    row = (plane * Y_SIZE + kappa // per_dev) * share + (kappa % per_dev) * 2 + part
                    for lane in range(cols // LANES):
                        turned[lane, pl.ds(row, z_size, stride=block), :] = result[
                            first : first + z_size, lane * LANES : (lane + 1) * LANES
                        ]
        if pair == 4:
            copies += send(0, 1, 0) + send(3, 1, PLANE)
    copies += send(1, 2, 2 * PLANE)
    for copy in copies:
        copy.wait()


def middle_kernel(plan, own, fft_len, keep_ref, volts_hbm, taps_hbm, table_hbm, out_ref, more_high, more_low, partial,
                  volts, taps, table, filt, high, low, turned, ready, out_sems, sems):
    rows = volts.shape[0]
    keep = keep_ref[0] != 0
    frames = volts.shape[1] // fft_len
    copies = [pltpu.make_async_copy(taps_hbm, taps, sems.at[0])]
    bounds = (0, 15, 21, 27, frames)
    for piece in range(4):
        part = pl.ds(bounds[piece] * fft_len, (bounds[piece + 1] - bounds[piece]) * fft_len)
        copies.append(pltpu.make_async_copy(volts_hbm.at[:, part], volts.at[:, part], sems.at[1 + piece]))
    copies.append(pltpu.make_async_copy(table_hbm, table, sems.at[5]))
    for copy in copies:
        copy.start()
    copies[0].wait()
    done = 0
    for piece in range(4):
        copies[1 + piece].wait()
        upto = bounds[piece + 1] - (taps.shape[0] - 1)
        filter_outputs(plan[done:upto], fft_len, keep, [volts], taps, None, filt, done)
        done = upto
    filter_outputs(own, fft_len, keep, [volts], taps, None, partial, 0)
    first_steps(filt, rows, 0, HALF, high, low, 0)
    first_steps(filt, rows, HALF, len(plan) - HALF, more_high, more_low, 0)
    copies[5].wait()
    second_steps(table, high, low, turned, ready, out_ref, 0, out_sems)


def edge_kernel(plan, fft_len, taps_hbm, table_hbm, earlier, later, partial, more_high, more_low, _, out_ref,
                taps, table, filt, high, low, turned, ready, out_sems, sems):
    rows = earlier.shape[0]
    copies = [
        pltpu.make_async_copy(more_high, high.at[:, pl.ds(0, more_high.shape[1])], sems.at[0]),
        pltpu.make_async_copy(more_low, low.at[:, pl.ds(0, more_low.shape[1])], sems.at[1]),
        pltpu.make_async_copy(table_hbm, table, sems.at[2]),
    ]
    first = pltpu.make_async_copy(taps_hbm, taps, sems.at[3])
    first.start()
    for copy in copies:
        copy.start()
    first.wait()
    filter_outputs(plan, fft_len, None, [earlier, later], taps, partial, filt, 0)
    first_steps(filt, rows, 0, len(plan), high, low, more_high.shape[1])
    for copy in copies:
        copy.wait()
    second_steps(table, high, low, turned, ready, out_ref, 1, out_sems)


def spectra_scratch(rows, fft_len, table, outputs):
    cols = HALF * rows
    return [
        pltpu.VMEM(table.shape, table.dtype),
        pltpu.VMEM((outputs * rows, fft_len), jnp.float32),
        pltpu.VMEM((RADIX // 2, cols, 2 * LANES), jnp.bfloat16),
        pltpu.VMEM((RADIX // 2, cols, 2 * LANES), jnp.bfloat16),
        pltpu.VMEM((cols // LANES, fft_len, LANES), jnp.float32),
        pltpu.VMEM((fft_len, cols), jnp.bfloat16),
        pltpu.SemaphoreType.DMA((3 * PLANE,)),
    ]


def middle_call(plan, own, keep, volts, taps, table):
    rows, fft_len = volts.shape[0], taps.shape[1]
    cols = HALF * rows
    more = jax.ShapeDtypeStruct((RADIX // 2, (len(plan) - HALF) * rows, 2 * LANES), jnp.bfloat16)
    partial = jax.ShapeDtypeStruct((len(own) * rows, fft_len), jnp.float32)
    hbm = pl.BlockSpec(memory_space=pltpu.HBM)
    vmem = pl.BlockSpec(memory_space=pltpu.VMEM)
    return pl.pallas_call(
        functools.partial(middle_kernel, plan, own, fft_len),
        out_shape=(pltpu.HBM((fft_len, 2 * cols), jnp.bfloat16), more, more, partial),
        in_specs=[pl.BlockSpec(memory_space=pltpu.SMEM), hbm, hbm, hbm],
        out_specs=(hbm, vmem, vmem, vmem),
        scratch_shapes=[pltpu.VMEM(volts.shape, volts.dtype), pltpu.VMEM(taps.shape, taps.dtype)]
        + spectra_scratch(rows, fft_len, table, len(plan))
        + [pltpu.SemaphoreType.DMA((6,))],
        compiler_params=pltpu.CompilerParams(vmem_limit_bytes=VMEM_LIMIT),
        cost_estimate=pl.CostEstimate(flops=10**9, bytes_accessed=8 * 2**20, transcendentals=0),
        name="middle",
    )(keep, *(pltpu.with_memory_space_constraint(x, pltpu.HBM) for x in (volts, taps, table)))


def edge_call(plan, taps, table, earlier, later, partial, more_high, more_low, spectra):
    rows, fft_len = earlier.shape[0], taps.shape[1]
    hbm = pl.BlockSpec(memory_space=pltpu.HBM)
    vmem = pl.BlockSpec(memory_space=pltpu.VMEM)
    anywhere = pl.BlockSpec(memory_space=pl.ANY)
    return pl.pallas_call(
        functools.partial(edge_kernel, plan, fft_len),
        out_shape=pltpu.HBM(spectra.shape, spectra.dtype),
        in_specs=[anywhere, anywhere, vmem, vmem, vmem, anywhere, anywhere, hbm],
        out_specs=hbm,
        scratch_shapes=[pltpu.VMEM(taps.shape, taps.dtype)]
        + spectra_scratch(rows, fft_len, table, len(plan))
        + [pltpu.SemaphoreType.DMA((4,))],
        input_output_aliases={7: 0},
        compiler_params=pltpu.CompilerParams(vmem_limit_bytes=VMEM_LIMIT),
        cost_estimate=pl.CostEstimate(flops=10**9, bytes_accessed=8 * 2**20, transcendentals=0),
        name="edge",
    )(
        taps, table, earlier, later, partial, more_high, more_low, spectra,
    )


def ends_kernel(volts, last_ref, first_ref, sems):
    size = last_ref.shape[1]
    copies = [
        pltpu.make_async_copy(volts.at[:, pl.ds(volts.shape[1] - size, size)], last_ref, sems.at[0]),
        pltpu.make_async_copy(volts.at[:, pl.ds(0, first_ref.shape[1])], first_ref, sems.at[1]),
    ]
    for copy in copies:
        copy.start()
    for copy in copies:
        copy.wait()


def ends_call(volts, last, first):
    vmem = pl.BlockSpec(memory_space=pltpu.VMEM)
    rows = volts.shape[0]
    return pl.pallas_call(
        ends_kernel,
        out_shape=(pltpu.VMEM((rows, last), volts.dtype), pltpu.VMEM((rows, first), volts.dtype)),
        in_specs=[pl.BlockSpec(memory_space=pltpu.HBM)],
        out_specs=(vmem, vmem),
        scratch_shapes=[pltpu.SemaphoreType.DMA((2,))],
        name="ends",
    )(pltpu.with_memory_space_constraint(volts, pltpu.HBM))


def gram_kernel(scale, pairs_ref, got_ref, out_ref, wide, both, tiles, sems):
    groups = wide.shape[0]
    per_src = 8
    times = Y_SIZE * Z_LOW
    inputs = LANES // 8
    pitch = 3 * per_src
    stations = Z_HIGH * PLANE * inputs

    @pl.loop(0, got_ref.shape[0] // (2 * per_src), unroll=8)
    def _(two):
        from_rows = pl.ds(pl.multiple_of(two * 2 * per_src, 2 * per_src), 2 * per_src)
        to_rows = pl.ds(pl.multiple_of(two * pitch, per_src), 2 * per_src)
        for group in range(groups):
            wide[group, to_rows] = got_ref[from_rows, group * LANES : (group + 1) * LANES].astype(jnp.float32)

    copies = []
    for chan in range(out_ref.shape[1]):
        for stn in range(Z_HIGH * PLANE):
            at = pl.ds(stn * inputs, inputs)
            turned_at = pl.ds(stations + stn * inputs, inputs)
            first = (stn % PLANE) * times * pitch + (stn // PLANE) * per_src + chan * 2
            parts = [
                [wide[group, pl.ds(first + part, times, stride=pitch), :] for group in range(groups)] for part in range(2)
            ]
            plain = jnp.concatenate(parts[0] + parts[1], 0).astype(jnp.bfloat16).T
            turned = jnp.concatenate([-v for v in parts[1]] + parts[0], 0).astype(jnp.bfloat16).T
            for t in range(LANES // inputs):
                cols = slice(t * LANES, (t + 1) * LANES)
                both[chan, at, cols] = plain[t * inputs : (t + 1) * inputs]
                both[chan, turned_at, cols] = turned[t * inputs : (t + 1) * inputs]
        sums = lax.dot_general(
            both[chan, :stations], both[chan], (((1,), (1,)), ((), ())), preferred_element_type=jnp.float32
        )
        for first in range(2):
            for second in range(2):
                for part in range(2):
                    col = part * stations + second * TILE
                    tiles[chan, first, second, part] = sums[first * TILE : (first + 1) * TILE, col : col + TILE] * scale
        for tile in range(pairs_ref.shape[0]):
            for part in range(2):
                copies.append(
                    pltpu.make_async_copy(
                        tiles.at[chan, pairs_ref[tile, 0], pairs_ref[tile, 1], part],
                        out_ref.at[part, chan, tile],
                        sems.at[len(copies)],
                    )
                )
                copies[-1].start()
    for copy in copies:
        copy.wait()


def gram_call(got, tile_pairs, chans, total_spectra):
    rows, lanes = got.shape
    stations = 2 * TILE
    depth = 8 * LANES
    tiles = tile_pairs.shape[0]
    return pl.pallas_call(
        functools.partial(gram_kernel, 1.0 / total_spectra),
        out_shape=jax.ShapeDtypeStruct((2, chans, tiles, TILE, TILE), jnp.float32),
        in_specs=[pl.BlockSpec(memory_space=pltpu.SMEM), pl.BlockSpec(memory_space=pltpu.VMEM)],
        out_specs=pl.BlockSpec(memory_space=pl.ANY),
        scratch_shapes=[
            pltpu.VMEM((lanes // LANES, rows // 2 * 3, LANES), jnp.float32),
            pltpu.VMEM((chans, 2 * stations, depth), jnp.bfloat16),
            pltpu.VMEM((chans, 2, 2, 2, TILE, TILE), jnp.float32),
            pltpu.SemaphoreType.DMA((2 * chans * tiles,)),
        ],
        compiler_params=pltpu.CompilerParams(vmem_limit_bytes=VMEM_LIMIT),
        name="grams",
    )(tile_pairs, got)


def plans(frames, tap_count):
    ahead = tap_count - 1 - BACK

    def taps(out):
        own, others = [], []
        for j in range(tap_count):
            frame = out - (tap_count - 1) + j
            if frame < 0:
                others.append((j, 0, frame + ahead, False))
            elif frame >= frames:
                others.append((j, 1, frame - frames, False))
            else:
                own.append((j, 0, frame, out >= frames))
        return own, others

    middle = [taps(out)[0] for out in range(tap_count - 1, frames)]
    edges = [taps(out) for out in [*range(BACK, tap_count - 1), *range(frames, frames + BACK)]]
    return middle, [own for own, _ in edges], [others for _, others in edges]


def shards(volts, taps, tile_pairs):
    tap_count, fft_len = taps.shape
    frames = volts.shape[1] // fft_len
    peers = lax.axis_size("tm")
    last, first = ends_call(volts, (tap_count - 1 - BACK) * fft_len, BACK * fft_len)
    earlier = lax.ppermute(last, "tm", [(i, i + 1) for i in range(peers - 1)])
    later = lax.ppermute(first, "tm", [(i, (i - 1) % peers) for i in range(peers)])
    table = jnp.asarray(second_step_table(fft_len))
    middle, own, others = plans(frames, tap_count)
    keep = (lax.axis_index("tm") != peers - 1).astype(jnp.int32).reshape(1)
    spectra, more_high, more_low, partial = middle_call(middle, own, keep, volts, taps, table)
    spectra = edge_call(others, taps, table, earlier, later, partial, more_high, more_low, spectra)
    order = device_order()
    chans = fft_len // 2 // len(order)
    blocks = spectra.reshape(len(order), 2 * chans, spectra.shape[1])
    got = lax.all_to_all(
        blocks, ("stn", "tm"), split_axis=0, concat_axis=0, tiled=True, axis_index_groups=[order]
    )
    return gram_call(got.reshape(spectra.shape), tile_pairs, chans, frames * peers)


def solution(mesh):
    return jax.shard_map(
        shards,
        mesh=mesh,
        in_specs=(P("stn", "tm"), P(), P()),
        out_specs=P(None, ("stn", "tm"), None, None, None),
        check_vma=False,
    )
```

time: 93.8 us -> 90.5 us (0.965)
  local copies, waits for them, and re-layouts: 2.6 us -> 0.11 us
    unnamed x9 -> x7, local copies, waits for them, and re-layouts: 2.6 us -> 0.11 us
  transfers between devices with their start and end apart: 3 -> 3, of which waited for: 1 -> 1; matrix products, arithmetic and copies ran while one was open for 0% -> 0% of each run, Pallas kernels for 6% -> 10%
where the time goes in v3:
time: 90.5 us; the launch traced here: 90.4 us
  waiting for transfers between devices  52.4 us (58%)
  starting transfers between devices  20.6 us (23%)
  Pallas kernels  17.1 us (19%)
    all_to_all x1, waiting for transfers between devices, shards(): lax.all_to_all(blocks, ('stn', 'tm'), split_axis=0, concat_axis=0, tiled=...  52.4 us
    all_to_all x1, starting transfers between devices, shards(): lax.all_to_all(blocks, ('stn', 'tm'), split_axis=0, concat_axis=0, tiled=...  11.6 us
    pallas_call x1, Pallas kernels, middle_call(): pl.pallas_call(functools.partial(middle_kernel, plan, own, fft_len), out_...  8.75 us
    ppermute x1, starting transfers between devices, shards(): lax.ppermute(first, 'tm', [(i, (i - 1) % peers) for i in range(peers)])  4.94 us
    ppermute x1, starting transfers between devices, shards(): earlier = lax.ppermute(last, 'tm', [(i, i + 1) for i in range(peers - 1)])  4.05 us
    pallas_call x1, Pallas kernels, edge_call(): pl.pallas_call(functools.partial(edge_kernel, plan, fft_len), out_shape=p...  3.66 us
    pallas_call x1, Pallas kernels, gram_call(): pl.pallas_call(functools.partial(gram_kernel, 1.0 / total_spectra), out_s...  3.57 us
  transfers between devices with their start and end apart: 3, of which 1 were waited for; matrix products, arithmetic and copies ran while one was open for 0% of the time, Pallas kernels for 10%

profile of v3, /device:TPU:1, one launch (start us, length us, event | category | flops | bytes accessed | tf_op | source)
XLA Modules:
  0.0 90.4 jit_solution(15185462580636067231)
XLA Ops:
  0.0 1.1 %ends.1 = (bf16[16,12288]{1,0:T(8,128)(2,1)S(1)}, bf16[16,10240]{1,0:T(8,128)(2,1)S(1)}) custom-call(bf16[16,65536]{1,0:T(8,128)(2,1)} %volts_hbm.1), custom_call_target="tpu_custom_call" | custom-call | tf_op jit(solution)/shard_map/ends/pallas_call | solution.py:300
  1.1 4.1 %collective-permute-start = (bf16[16,12288]{1,0:T(8,128)(2,1)S(1)}, bf16[16,12288]{1,0:T(8,128)(2,1)S(1)}, u32[]{:S(2)}, u32[]{:S(2)}) collective-permute-start(bf16[16,12288]{1,0:T(8,128)(2,1)S(1)} %get-tuple-element.11), channel_id=1, source_target_pairs={{0,1},{1,2},{2,3},{3,4},{4,5},{5,6},{6,7},{7,8},{8,9},{9,10},{10,1... | collective-permute-start | bytes 1179656 | tf_op jit(solution)/shard_map/ppermute | solution.py:408
  5.2 4.9 %collective-permute-start.1 = (bf16[16,10240]{1,0:T(8,128)(2,1)S(1)}, bf16[16,10240]{1,0:T(8,128)(2,1)S(1)}, u32[]{:S(2)}, u32[]{:S(2)}) collective-permute-start(bf16[16,10240]{1,0:T(8,128)(2,1)S(1)} %get-tuple-element.12), channel_id=1, source_target_pairs={{0,15},{1,0},{2,1},{3,2},{4,3},{5,4},{6,5},{7,6},{8,7},{9,8},{10,9... | collective-permute-start | bytes 983048 | tf_op jit(solution)/shard_map/ppermute | solution.py:409
  10.1 0.0 copy-start
  10.1 0.0 copy-start.1
  10.1 8.7 %middle.1 = (bf16[2048,512]{1,0:T(8,128)(2,1)}, bf16[8,80,256]{2,1,0:T(8,128)(2,1)S(1)}, bf16[8,80,256]{2,1,0:T(8,128)(2,1)S(1)}, f32[176,2048]{1,0:T(8,128)S(1)}) custom-call(s32[1]{0:T(128)} %bitcast.keep_ref, bf16[16,65536]{1,0:T(8,128)(2,1)} %volts_hbm.1, f32[12,2048]{1,0:T(8,128)} %taps_hbm.3, bf16[8,512,256]{2,1,0:T(8,128)(2,1)} %constant.8.clone.table_hbm), custom_call_target="tpu_custom_call" | custom-call | flops 1000000000 | bytes 8388608 | tf_op jit(solution)/shard_map/middle/pallas_call | solution.py:249
  18.9 0.0 collective-permute-done.1.later
  18.9 0.0 collective-permute-done.earlier
  18.9 0.0 copy-done
  18.9 0.0 copy-done.1
  18.9 3.7 %edge.1 = bf16[2048,512]{1,0:T(8,128)(2,1)} custom-call(f32[12,2048]{1,0:T(8,128)S(1)} %copy-done.1, bf16[8,512,256]{2,1,0:T(8,128)(2,1)S(1)} %copy-done, bf16[16,12288]{1,0:T(8,128)(2,1)S(1)} %collective-permute-done.earlier, bf16[16,10240]{1,0:T(8,128)(2,1)S(1)} %collective-permute-done.1.later, ...), custom_call_target="tpu_custom_call", output_to_operand_aliasing={{}: (7, {})} | custom-call | flops 1000000000 | bytes 8388608 | tf_op jit(solution)/shard_map/edge/pallas_call | solution.py:268
  22.6 0.0 copy-start.2
  22.6 11.6 %all-to-all-start = ((bf16[256,8,512]{2,1,0:T(8,128)(2,1)}), bf16[256,8,512]{2,1,0:T(8,128)(2,1)S(1)}, u32[]{:S(2)}, u32[]{:S(2)}) async-start(bf16[256,8,512]{2,1,0:T(8,128)(2,1)} %bitcast.4), calls=%async_computation | async-start | bytes 4194304 | tf_op jit(solution)/shard_map/all_to_all | solution.py:418
  34.3 0.0 copy-done.2
  34.3 0.1 copy.6.pairs_ref
  34.4 52.4 %all-to-all-done = bf16[256,8,512]{2,1,0:T(8,128)(2,1)S(1)} async-done(((bf16[256,8,512]{2,1,0:T(8,128)(2,1)}), bf16[256,8,512]{2,1,0:T(8,128)(2,1)S(1)}, u32[]{:S(2)}, u32[]{:S(2)}) %all-to-all-start) | async-done | bytes 2097184 | tf_op jit(solution)/shard_map/all_to_all | solution.py:418
  86.8 3.6 %grams.1 = f32[2,4,3,128,128]{4,3,2,1,0:T(8,128)} custom-call(s32[3,2]{1,0:T(4,128)S(1)} %copy.6.pairs_ref, bf16[2048,512]{1,0:T(8,128)(2,1)S(1)} %bitcast.3), custom_call_target="tpu_custom_call" | custom-call | tf_op jit(solution)/shard_map/grams/pallas_call | solution.py:367
Async XLA Ops:
  1.1 17.8 %collective-permute-start = (bf16[16,12288]{1,0:T(8,128)(2,1)S(1)}, bf16[16,12288]{1,0:T(8,128)(2,1)S(1)}, u32[]{:S(2)}, u32[]{:S(2)}) collective-permute-start(bf16[16,12288]{1,0:T(8,128)(2,1)S(1)} %get-tuple-element.11), channel_id=1, source_target_pairs={{0,1},{1,2},{2,3},{3,4},{4,5},{5,6},{6,7},{7,8},{8,9},{9,10},{10,1... | collective-permute-start | bytes 1179656 | tf_op jit(solution)/shard_map/ppermute | solution.py:408
  5.2 13.7 %collective-permute-start.1 = (bf16[16,10240]{1,0:T(8,128)(2,1)S(1)}, bf16[16,10240]{1,0:T(8,128)(2,1)S(1)}, u32[]{:S(2)}, u32[]{:S(2)}) collective-permute-start(bf16[16,10240]{1,0:T(8,128)(2,1)S(1)} %get-tuple-element.12), channel_id=1, source_target_pairs={{0,15},{1,0},{2,1},{3,2},{4,3},{5,4},{6,5},{7,6},{8,7},{9,8},{10,9... | collective-permute-start | bytes 983048 | tf_op jit(solution)/shard_map/ppermute | solution.py:409
  10.1 8.8 %copy-start = (bf16[8,512,256]{2,1,0:T(8,128)(2,1)S(1)}, bf16[8,512,256]{2,1,0:T(8,128)(2,1)}, u32[]{:S(2)}) copy-start(bf16[8,512,256]{2,1,0:T(8,128)(2,1)} %constant.8.clone.table_hbm) | copy-start | bytes 6291460
  10.1 8.8 %copy-start.1 = (f32[12,2048]{1,0:T(8,128)S(1)}, f32[12,2048]{1,0:T(8,128)}, u32[]{:S(2)}) copy-start(f32[12,2048]{1,0:T(8,128)} %taps_hbm.3) | copy-start | bytes 294916
  22.6 11.7 %copy-start.2 = (s32[3,2]{0,1:T(2,128)S(1)}, s32[3,2]{0,1:T(2,128)}, u32[]{:S(2)}) copy-start(s32[3,2]{0,1:T(2,128)} %param.6) | copy-start | bytes 76
  22.6 64.2 %all-to-all-start = ((bf16[256,8,512]{2,1,0:T(8,128)(2,1)}), bf16[256,8,512]{2,1,0:T(8,128)(2,1)S(1)}, u32[]{:S(2)}, u32[]{:S(2)}) async-start(bf16[256,8,512]{2,1,0:T(8,128)(2,1)} %bitcast.4), calls=%async_computation | async-start | bytes 4194304 | tf_op jit(solution)/shard_map/all_to_all | solution.py:418

commit v4 on v3

--- a/solution.py
+++ b/solution.py
@@ -180,7 +180,7 @@
 
 
 def middle_kernel(plan, own, fft_len, keep_ref, volts_hbm, taps_hbm, table_hbm, out_ref, more_high, more_low, partial,
-                  volts, taps, table, filt, high, low, turned, ready, out_sems, sems):
+                  taps, table, volts, filt, high, low, turned, ready, out_sems, sems):
     rows = volts.shape[0]
     keep = keep_ref[0] != 0
     frames = volts.shape[1] // fft_len
@@ -206,19 +206,15 @@
     second_steps(table, high, low, turned, ready, out_ref, 0, out_sems)
 
 
-def edge_kernel(plan, fft_len, taps_hbm, table_hbm, earlier, later, partial, more_high, more_low, _, out_ref,
-                taps, table, filt, high, low, turned, ready, out_sems, sems):
+def edge_kernel(plan, fft_len, taps, table, earlier, later, partial, more_high, more_low, _, out_ref,
+                filt, high, low, turned, ready, out_sems, sems):
     rows = earlier.shape[0]
     copies = [
         pltpu.make_async_copy(more_high, high.at[:, pl.ds(0, more_high.shape[1])], sems.at[0]),
         pltpu.make_async_copy(more_low, low.at[:, pl.ds(0, more_low.shape[1])], sems.at[1]),
-        pltpu.make_async_copy(table_hbm, table, sems.at[2]),
     ]
-    first = pltpu.make_async_copy(taps_hbm, taps, sems.at[3])
-    first.start()
     for copy in copies:
         copy.start()
-    first.wait()
     filter_outputs(plan, fft_len, None, [earlier, later], taps, partial, filt, 0)
     first_steps(filt, rows, 0, len(plan), high, low, more_high.shape[1])
     for copy in copies:
@@ -226,10 +222,9 @@
     second_steps(table, high, low, turned, ready, out_ref, 1, out_sems)
 
 
-def spectra_scratch(rows, fft_len, table, outputs):
+def spectra_scratch(rows, fft_len, outputs):
     cols = HALF * rows
     return [
-        pltpu.VMEM(table.shape, table.dtype),
         pltpu.VMEM((outputs * rows, fft_len), jnp.float32),
         pltpu.VMEM((RADIX // 2, cols, 2 * LANES), jnp.bfloat16),
         pltpu.VMEM((RADIX // 2, cols, 2 * LANES), jnp.bfloat16),
@@ -248,11 +243,14 @@
     vmem = pl.BlockSpec(memory_space=pltpu.VMEM)
     return pl.pallas_call(
         functools.partial(middle_kernel, plan, own, fft_len),
-        out_shape=(pltpu.HBM((fft_len, 2 * cols), jnp.bfloat16), more, more, partial),
+        out_shape=(
+            pltpu.HBM((fft_len, 2 * cols), jnp.bfloat16),
+            *(pltpu.VMEM(x.shape, x.dtype) for x in (more, more, partial, taps, table)),
+        ),
         in_specs=[pl.BlockSpec(memory_space=pltpu.SMEM), hbm, hbm, hbm],
-        out_specs=(hbm, vmem, vmem, vmem),
-        scratch_shapes=[pltpu.VMEM(volts.shape, volts.dtype), pltpu.VMEM(taps.shape, taps.dtype)]
-        + spectra_scratch(rows, fft_len, table, len(plan))
+        out_specs=(hbm, vmem, vmem, vmem, vmem, vmem),
+        scratch_shapes=[pltpu.VMEM(volts.shape, volts.dtype)]
+        + spectra_scratch(rows, fft_len, len(plan))
         + [pltpu.SemaphoreType.DMA((6,))],
         compiler_params=pltpu.CompilerParams(vmem_limit_bytes=VMEM_LIMIT),
         cost_estimate=pl.CostEstimate(flops=10**9, bytes_accessed=8 * 2**20, transcendentals=0),
@@ -268,11 +266,9 @@
     return pl.pallas_call(
         functools.partial(edge_kernel, plan, fft_len),
         out_shape=pltpu.HBM(spectra.shape, spectra.dtype),
-        in_specs=[anywhere, anywhere, vmem, vmem, vmem, anywhere, anywhere, hbm],
+        in_specs=[vmem, vmem, vmem, vmem, vmem, anywhere, anywhere, hbm],
         out_specs=hbm,
-        scratch_shapes=[pltpu.VMEM(taps.shape, taps.dtype)]
-        + spectra_scratch(rows, fft_len, table, len(plan))
-        + [pltpu.SemaphoreType.DMA((4,))],
+        scratch_shapes=spectra_scratch(rows, fft_len, len(plan)) + [pltpu.SemaphoreType.DMA((2,))],
         input_output_aliases={7: 0},
         compiler_params=pltpu.CompilerParams(vmem_limit_bytes=VMEM_LIMIT),
         cost_estimate=pl.CostEstimate(flops=10**9, bytes_accessed=8 * 2**20, transcendentals=0),
@@ -315,16 +311,16 @@
     pitch = 3 * per_src
     stations = Z_HIGH * PLANE * inputs
 
-    @pl.loop(0, got_ref.shape[0] // (2 * per_src), unroll=8)
-    def _(two):
-        from_rows = pl.ds(pl.multiple_of(two * 2 * per_src, 2 * per_src), 2 * per_src)
-        to_rows = pl.ds(pl.multiple_of(two * pitch, per_src), 2 * per_src)
-        for group in range(groups):
-            wide[group, to_rows] = got_ref[from_rows, group * LANES : (group + 1) * LANES].astype(jnp.float32)
-
     copies = []
     for chan in range(out_ref.shape[1]):
         for stn in range(Z_HIGH * PLANE):
+            if chan == 0 and stn < PLANE:
+                for two in range(stn * times, (stn + 1) * times):
+                    from_rows = pl.ds(two * 2 * per_src, 2 * per_src)
+                    for group in range(groups):
+                        wide[group, pl.ds(two * pitch, 2 * per_src)] = got_ref[
+                            from_rows, group * LANES : (group + 1) * LANES
+                        ].astype(jnp.float32)
             at = pl.ds(stn * inputs, inputs)
             turned_at = pl.ds(stations + stn * inputs, inputs)
             first = (stn % PLANE) * times * pitch + (stn // PLANE) * per_src + chan * 2
@@ -410,7 +406,7 @@
     table = jnp.asarray(second_step_table(fft_len))
     middle, own, others = plans(frames, tap_count)
     keep = (lax.axis_index("tm") != peers - 1).astype(jnp.int32).reshape(1)
-    spectra, more_high, more_low, partial = middle_call(middle, own, keep, volts, taps, table)
+    spectra, more_high, more_low, partial, taps, table = middle_call(middle, own, keep, volts, taps, table)
     spectra = edge_call(others, taps, table, earlier, later, partial, more_high, more_low, spectra)
     order = device_order()
     chans = fft_len // 2 // len(order)

time: 90.5 us -> 90.1 us (level)
  no operation moved by 1% of the time
where the time goes in v4:
time: 90.1 us; the launch traced here: 89.9 us
  waiting for transfers between devices  52.4 us (58%)
  starting transfers between devices  20.8 us (23%)
  Pallas kernels  16.5 us (18%)
    all_to_all x1, waiting for transfers between devices, shards(): lax.all_to_all(blocks, ('stn', 'tm'), split_axis=0, concat_axis=0, tiled=...  52.4 us
    all_to_all x1, starting transfers between devices, shards(): lax.all_to_all(blocks, ('stn', 'tm'), split_axis=0, concat_axis=0, tiled=...  11.8 us
    pallas_call x1, Pallas kernels, middle_call(): pl.pallas_call(functools.partial(middle_kernel, plan, own, fft_len), out_...  8.57 us
    ppermute x1, starting transfers between devices, shards(): lax.ppermute(first, 'tm', [(i, (i - 1) % peers) for i in range(peers)])  4.94 us
    ppermute x1, starting transfers between devices, shards(): earlier = lax.ppermute(last, 'tm', [(i, i + 1) for i in range(peers - 1)])  4.05 us
    pallas_call x1, Pallas kernels, gram_call(): pl.pallas_call(functools.partial(gram_kernel, 1.0 / total_spectra), out_s...  3.46 us
    pallas_call x1, Pallas kernels, edge_call(): pl.pallas_call(functools.partial(edge_kernel, plan, fft_len), out_shape=p...  3.36 us
  transfers between devices with their start and end apart: 3, of which 1 were waited for; matrix products, arithmetic and copies ran while one was open for 0% of the time, Pallas kernels for 10%

profile of v4, /device:TPU:1, one launch (start us, length us, event | category | flops | bytes accessed | tf_op | source)
XLA Modules:
  0.0 89.9 jit_solution(1380743712748524038)
XLA Ops:
  0.0 1.1 %ends.1 = (bf16[16,12288]{1,0:T(8,128)(2,1)S(1)}, bf16[16,10240]{1,0:T(8,128)(2,1)S(1)}) custom-call(bf16[16,65536]{1,0:T(8,128)(2,1)} %volts.1), custom_call_target="tpu_custom_call" | custom-call | tf_op jit(solution)/shard_map/ends/pallas_call | solution.py:296
  1.1 4.1 %collective-permute-start = (bf16[16,12288]{1,0:T(8,128)(2,1)S(1)}, bf16[16,12288]{1,0:T(8,128)(2,1)S(1)}, u32[]{:S(2)}, u32[]{:S(2)}) collective-permute-start(bf16[16,12288]{1,0:T(8,128)(2,1)S(1)} %get-tuple-element.15), channel_id=1, source_target_pairs={{0,1},{1,2},{2,3},{3,4},{4,5},{5,6},{6,7},{7,8},{8,9},{9,10},{10,1... | collective-permute-start | bytes 1179656 | tf_op jit(solution)/shard_map/ppermute | solution.py:404
  5.2 4.9 %collective-permute-start.1 = (bf16[16,10240]{1,0:T(8,128)(2,1)S(1)}, bf16[16,10240]{1,0:T(8,128)(2,1)S(1)}, u32[]{:S(2)}, u32[]{:S(2)}) collective-permute-start(bf16[16,10240]{1,0:T(8,128)(2,1)S(1)} %get-tuple-element.16), channel_id=1, source_target_pairs={{0,15},{1,0},{2,1},{3,2},{4,3},{5,4},{6,5},{7,6},{8,7},{9,8},{10,9... | collective-permute-start | bytes 983048 | tf_op jit(solution)/shard_map/ppermute | solution.py:405
  10.1 8.6 %middle.1 = (bf16[2048,512]{1,0:T(8,128)(2,1)}, bf16[8,80,256]{2,1,0:T(8,128)(2,1)S(1)}, bf16[8,80,256]{2,1,0:T(8,128)(2,1)S(1)}, f32[176,2048]{1,0:T(8,128)S(1)...) custom-call(s32[1]{0:T(128)} %bitcast.keep_ref, bf16[16,65536]{1,0:T(8,128)(2,1)} %volts.1, ...), custom_call_target="tpu_custom_call" | custom-call | flops 1000000000 | bytes 8388608 | tf_op jit(solution)/shard_map/middle/pallas_call | solution.py:244
  18.7 0.0 collective-permute-done.1.later
  18.7 0.0 collective-permute-done.earlier
  18.7 3.4 %edge.1 = bf16[2048,512]{1,0:T(8,128)(2,1)} custom-call(f32[12,2048]{1,0:T(8,128)S(1)} %get-tuple-element.13.taps, bf16[8,512,256]{2,1,0:T(8,128)(2,1)S(1)} %get-tuple-element.14.table, bf16[16,12288]{1,0:T(8,128)(2,1)S(1)} %collective-permute-done.earlier, bf16[16,10240]{1,0:T(8,128)(2,1)S(1)} %collective-permute-done.1.later, ...), custom_call_target="tpu_custom_call", output_to_operand_aliasing={{}: (7, {})} | custom-call | flops 1000000000 | bytes 8388608 | tf_op jit(solution)/shard_map/edge/pallas_call | solution.py:266
  22.1 0.0 copy-start
  22.1 11.8 %all-to-all-start = ((bf16[256,8,512]{2,1,0:T(8,128)(2,1)}), bf16[256,8,512]{2,1,0:T(8,128)(2,1)S(1)}, u32[]{:S(2)}, u32[]{:S(2)}) async-start(bf16[256,8,512]{2,1,0:T(8,128)(2,1)} %bitcast.4), calls=%async_computation | async-start | bytes 4194304 | tf_op jit(solution)/shard_map/all_to_all | solution.py:414
  33.9 0.0 copy-done
  33.9 0.1 copy.6.pairs_ref
  34.0 52.4 %all-to-all-done = bf16[256,8,512]{2,1,0:T(8,128)(2,1)S(1)} async-done(((bf16[256,8,512]{2,1,0:T(8,128)(2,1)}), bf16[256,8,512]{2,1,0:T(8,128)(2,1)S(1)}, u32[]{:S(2)}, u32[]{:S(2)}) %all-to-all-start) | async-done | bytes 2097184 | tf_op jit(solution)/shard_map/all_to_all | solution.py:414
  86.5 3.5 %grams.1 = f32[2,4,3,128,128]{4,3,2,1,0:T(8,128)} custom-call(s32[3,2]{1,0:T(4,128)S(1)} %copy.6.pairs_ref, bf16[2048,512]{1,0:T(8,128)(2,1)S(1)} %bitcast.3), custom_call_target="tpu_custom_call" | custom-call | tf_op jit(solution)/shard_map/grams/pallas_call | solution.py:363
Async XLA Ops:
  1.1 17.6 %collective-permute-start = (bf16[16,12288]{1,0:T(8,128)(2,1)S(1)}, bf16[16,12288]{1,0:T(8,128)(2,1)S(1)}, u32[]{:S(2)}, u32[]{:S(2)}) collective-permute-start(bf16[16,12288]{1,0:T(8,128)(2,1)S(1)} %get-tuple-element.15), channel_id=1, source_target_pairs={{0,1},{1,2},{2,3},{3,4},{4,5},{5,6},{6,7},{7,8},{8,9},{9,10},{10,1... | collective-permute-start | bytes 1179656 | tf_op jit(solution)/shard_map/ppermute | solution.py:404
  5.2 13.5 %collective-permute-start.1 = (bf16[16,10240]{1,0:T(8,128)(2,1)S(1)}, bf16[16,10240]{1,0:T(8,128)(2,1)S(1)}, u32[]{:S(2)}, u32[]{:S(2)}) collective-permute-start(bf16[16,10240]{1,0:T(8,128)(2,1)S(1)} %get-tuple-element.16), channel_id=1, source_target_pairs={{0,15},{1,0},{2,1},{3,2},{4,3},{5,4},{6,5},{7,6},{8,7},{9,8},{10,9... | collective-permute-start | bytes 983048 | tf_op jit(solution)/shard_map/ppermute | solution.py:405
  22.1 11.9 %copy-start = (s32[3,2]{0,1:T(2,128)S(1)}, s32[3,2]{0,1:T(2,128)}, u32[]{:S(2)}) copy-start(s32[3,2]{0,1:T(2,128)} %param.6) | copy-start | bytes 76
  22.1 64.4 %all-to-all-start = ((bf16[256,8,512]{2,1,0:T(8,128)(2,1)}), bf16[256,8,512]{2,1,0:T(8,128)(2,1)S(1)}, u32[]{:S(2)}, u32[]{:S(2)}) async-start(bf16[256,8,512]{2,1,0:T(8,128)(2,1)} %bitcast.4), calls=%async_computation | async-start | bytes 4194304 | tf_op jit(solution)/shard_map/all_to_all | solution.py:414

commit v5 on v4

--- a/solution.py
+++ b/solution.py
@@ -119,8 +119,8 @@
                 out_ref[at, lanes] = total
 
 
-def first_steps(filt, rows, first, count, high, low, offset):
-    @pl.loop(0, count)
+def first_steps(filt, rows, first, count, high, low, offset, unroll=1):
+    @pl.loop(0, count, unroll=unroll)
     def _(out):
         at = pl.ds(pl.multiple_of((out + first) * rows, rows), rows)
         to = pl.ds(pl.multiple_of(out * rows + offset, rows), rows)
@@ -159,9 +159,8 @@
     copies = []
     for pair in range(RADIX // 2):
         table_high, table_low = table[pair, :size], table[pair, size:]
-        result = (
-            product(table_high, low[pair]) + product(table_low, high[pair])
-        ) + product(table_high, high[pair])
+        both = product(table[pair], high[pair])
+        result = (both[size:] + product(table_high, low[pair])) + both[:size]
         for slot in range(2):
             kappa = (pair, RADIX - pair)[slot] if pair else (0, RADIX // 2)[slot]
             for part in range(2):
@@ -216,7 +215,7 @@
     for copy in copies:
         copy.start()
     filter_outputs(plan, fft_len, None, [earlier, later], taps, partial, filt, 0)
-    first_steps(filt, rows, 0, len(plan), high, low, more_high.shape[1])
+    first_steps(filt, rows, 0, len(plan), high, low, more_high.shape[1], len(plan))
     for copy in copies:
         copy.wait()
     second_steps(table, high, low, turned, ready, out_ref, 1, out_sems)
@@ -228,7 +227,7 @@
         pltpu.VMEM((outputs * rows, fft_len), jnp.float32),
         pltpu.VMEM((RADIX // 2, cols, 2 * LANES), jnp.bfloat16),
         pltpu.VMEM((RADIX // 2, cols, 2 * LANES), jnp.bfloat16),
-        pltpu.VMEM((cols // LANES, fft_len, LANES), jnp.float32),
+        pltpu.VMEM((cols // LANES, fft_len + 8, LANES), jnp.float32),
         pltpu.VMEM((fft_len, cols), jnp.bfloat16),
         pltpu.SemaphoreType.DMA((3 * PLANE,)),
     ]
@@ -366,7 +365,7 @@
         in_specs=[pl.BlockSpec(memory_space=pltpu.SMEM), pl.BlockSpec(memory_space=pltpu.VMEM)],
         out_specs=pl.BlockSpec(memory_space=pl.ANY),
         scratch_shapes=[
-            pltpu.VMEM((lanes // LANES, rows // 2 * 3, LANES), jnp.float32),
+            pltpu.VMEM((lanes // LANES, rows // 2 * 3 + 24, LANES), jnp.float32),
             pltpu.VMEM((chans, 2 * stations, depth), jnp.bfloat16),
             pltpu.VMEM((chans, 2, 2, 2, TILE, TILE), jnp.float32),
             pltpu.SemaphoreType.DMA((2 * chans * tiles,)),

time: 90.1 us -> 90 us (level)
  no operation moved by 1% of the time
where the time goes in v5:
time: 90 us; the launch traced here: 89.8 us
  waiting for transfers between devices  52.4 us (58%)
  starting transfers between devices  20.9 us (23%)
  Pallas kernels  16.3 us (18%)
    all_to_all x1, waiting for transfers between devices, shards(): lax.all_to_all(blocks, ('stn', 'tm'), split_axis=0, concat_axis=0, tiled=...  52.4 us
    all_to_all x1, starting transfers between devices, shards(): lax.all_to_all(blocks, ('stn', 'tm'), split_axis=0, concat_axis=0, tiled=...  11.9 us
    pallas_call x1, Pallas kernels, middle_call(): pl.pallas_call(functools.partial(middle_kernel, plan, own, fft_len), out_...  8.53 us
    ppermute x1, starting transfers between devices, shards(): lax.ppermute(first, 'tm', [(i, (i - 1) % peers) for i in range(peers)])  4.94 us
    ppermute x1, starting transfers between devices, shards(): earlier = lax.ppermute(last, 'tm', [(i, i + 1) for i in range(peers - 1)])  4.05 us
    pallas_call x1, Pallas kernels, gram_call(): pl.pallas_call(functools.partial(gram_kernel, 1.0 / total_spectra), out_s...  3.46 us
    pallas_call x1, Pallas kernels, edge_call(): pl.pallas_call(functools.partial(edge_kernel, plan, fft_len), out_shape=p...  3.25 us
  transfers between devices with their start and end apart: 3, of which 1 were waited for; matrix products, arithmetic and copies ran while one was open for 0% of the time, Pallas kernels for 10%

profile of v5, /device:TPU:1, one launch (start us, length us, event | category | flops | bytes accessed | tf_op | source)
XLA Modules:
  0.0 89.8 jit_solution(10262251913501370554)
XLA Ops:
  0.0 1.1 %ends.1 = (bf16[16,12288]{1,0:T(8,128)(2,1)S(1)}, bf16[16,10240]{1,0:T(8,128)(2,1)S(1)}) custom-call(bf16[16,65536]{1,0:T(8,128)(2,1)} %volts.1), custom_call_target="tpu_custom_call" | custom-call | tf_op jit(solution)/shard_map/ends/pallas_call | solution.py:295
  1.1 4.1 %collective-permute-start = (bf16[16,12288]{1,0:T(8,128)(2,1)S(1)}, bf16[16,12288]{1,0:T(8,128)(2,1)S(1)}, u32[]{:S(2)}, u32[]{:S(2)}) collective-permute-start(bf16[16,12288]{1,0:T(8,128)(2,1)S(1)} %get-tuple-element.15), channel_id=1, source_target_pairs={{0,1},{1,2},{2,3},{3,4},{4,5},{5,6},{6,7},{7,8},{8,9},{9,10},{10,1... | collective-permute-start | bytes 1179656 | tf_op jit(solution)/shard_map/ppermute | solution.py:403
  5.2 4.9 %collective-permute-start.1 = (bf16[16,10240]{1,0:T(8,128)(2,1)S(1)}, bf16[16,10240]{1,0:T(8,128)(2,1)S(1)}, u32[]{:S(2)}, u32[]{:S(2)}) collective-permute-start(bf16[16,10240]{1,0:T(8,128)(2,1)S(1)} %get-tuple-element.16), channel_id=1, source_target_pairs={{0,15},{1,0},{2,1},{3,2},{4,3},{5,4},{6,5},{7,6},{8,7},{9,8},{10,9... | collective-permute-start | bytes 983048 | tf_op jit(solution)/shard_map/ppermute | solution.py:404
  10.1 8.5 %middle.1 = (bf16[2048,512]{1,0:T(8,128)(2,1)}, bf16[8,80,256]{2,1,0:T(8,128)(2,1)S(1)}, bf16[8,80,256]{2,1,0:T(8,128)(2,1)S(1)}, f32[176,2048]{1,0:T(8,128)S(1)...) custom-call(s32[1]{0:T(128)} %bitcast.keep_ref, bf16[16,65536]{1,0:T(8,128)(2,1)} %volts.1, ...), custom_call_target="tpu_custom_call" | custom-call | flops 1000000000 | bytes 8388608 | tf_op jit(solution)/shard_map/middle/pallas_call | solution.py:243
  18.7 0.0 collective-permute-done.1.later
  18.7 0.0 collective-permute-done.earlier
  18.7 3.2 %edge.1 = bf16[2048,512]{1,0:T(8,128)(2,1)} custom-call(f32[12,2048]{1,0:T(8,128)S(1)} %get-tuple-element.13.taps, bf16[8,512,256]{2,1,0:T(8,128)(2,1)S(1)} %get-tuple-element.14.table, bf16[16,12288]{1,0:T(8,128)(2,1)S(1)} %collective-permute-done.earlier, bf16[16,10240]{1,0:T(8,128)(2,1)S(1)} %collective-permute-done.1.later, ...), custom_call_target="tpu_custom_call", output_to_operand_aliasing={{}: (7, {})} | custom-call | flops 1000000000 | bytes 8388608 | tf_op jit(solution)/shard_map/edge/pallas_call | solution.py:265
  21.9 0.0 copy-start
  21.9 11.9 %all-to-all-start = ((bf16[256,8,512]{2,1,0:T(8,128)(2,1)}), bf16[256,8,512]{2,1,0:T(8,128)(2,1)S(1)}, u32[]{:S(2)}, u32[]{:S(2)}) async-start(bf16[256,8,512]{2,1,0:T(8,128)(2,1)} %bitcast.4), calls=%async_computation | async-start | bytes 4194304 | tf_op jit(solution)/shard_map/all_to_all | solution.py:413
  33.8 0.0 copy-done
  33.8 0.1 copy.6.pairs_ref
  33.9 52.4 %all-to-all-done = bf16[256,8,512]{2,1,0:T(8,128)(2,1)S(1)} async-done(((bf16[256,8,512]{2,1,0:T(8,128)(2,1)}), bf16[256,8,512]{2,1,0:T(8,128)(2,1)S(1)}, u32[]{:S(2)}, u32[]{:S(2)}) %all-to-all-start) | async-done | bytes 2097184 | tf_op jit(solution)/shard_map/all_to_all | solution.py:413
  86.3 3.5 %grams.1 = f32[2,4,3,128,128]{4,3,2,1,0:T(8,128)} custom-call(s32[3,2]{1,0:T(4,128)S(1)} %copy.6.pairs_ref, bf16[2048,512]{1,0:T(8,128)(2,1)S(1)} %bitcast.3), custom_call_target="tpu_custom_call" | custom-call | tf_op jit(solution)/shard_map/grams/pallas_call | solution.py:362
Async XLA Ops:
  1.1 17.6 %collective-permute-start = (bf16[16,12288]{1,0:T(8,128)(2,1)S(1)}, bf16[16,12288]{1,0:T(8,128)(2,1)S(1)}, u32[]{:S(2)}, u32[]{:S(2)}) collective-permute-start(bf16[16,12288]{1,0:T(8,128)(2,1)S(1)} %get-tuple-element.15), channel_id=1, source_target_pairs={{0,1},{1,2},{2,3},{3,4},{4,5},{5,6},{6,7},{7,8},{8,9},{9,10},{10,1... | collective-permute-start | bytes 1179656 | tf_op jit(solution)/shard_map/ppermute | solution.py:403
  5.2 13.5 %collective-permute-start.1 = (bf16[16,10240]{1,0:T(8,128)(2,1)S(1)}, bf16[16,10240]{1,0:T(8,128)(2,1)S(1)}, u32[]{:S(2)}, u32[]{:S(2)}) collective-permute-start(bf16[16,10240]{1,0:T(8,128)(2,1)S(1)} %get-tuple-element.16), channel_id=1, source_target_pairs={{0,15},{1,0},{2,1},{3,2},{4,3},{5,4},{6,5},{7,6},{8,7},{9,8},{10,9... | collective-permute-start | bytes 983048 | tf_op jit(solution)/shard_map/ppermute | solution.py:404
  21.9 11.9 %copy-start = (s32[3,2]{0,1:T(2,128)S(1)}, s32[3,2]{0,1:T(2,128)}, u32[]{:S(2)}) copy-start(s32[3,2]{0,1:T(2,128)} %param.6) | copy-start | bytes 76
  21.9 64.4 %all-to-all-start = ((bf16[256,8,512]{2,1,0:T(8,128)(2,1)}), bf16[256,8,512]{2,1,0:T(8,128)(2,1)S(1)}, u32[]{:S(2)}, u32[]{:S(2)}) async-start(bf16[256,8,512]{2,1,0:T(8,128)(2,1)} %bitcast.4), calls=%async_computation | async-start | bytes 4194304 | tf_op jit(solution)/shard_map/all_to_all | solution.py:413

commit v6 on v5

--- a/solution.py
+++ b/solution.py
@@ -178,10 +178,10 @@
         copy.wait()
 
 
-def middle_kernel(plan, own, fft_len, keep_ref, volts_hbm, taps_hbm, table_hbm, out_ref, more_high, more_low, partial,
-                  taps, table, volts, filt, high, low, turned, ready, out_sems, sems):
+def middle_kernel(plan, own, fft_len, pairs_hbm, volts_hbm, taps_hbm, table_hbm, out_ref, more_high, more_low,
+                  partial, taps, table, pairs_out, volts, filt, high, low, turned, ready, out_sems, sems):
     rows = volts.shape[0]
-    keep = keep_ref[0] != 0
+    keep = lax.axis_index("tm") != lax.axis_size("tm") - 1
     frames = volts.shape[1] // fft_len
     copies = [pltpu.make_async_copy(taps_hbm, taps, sems.at[0])]
     bounds = (0, 15, 21, 27, frames)
@@ -189,6 +189,7 @@
         part = pl.ds(bounds[piece] * fft_len, (bounds[piece + 1] - bounds[piece]) * fft_len)
         copies.append(pltpu.make_async_copy(volts_hbm.at[:, part], volts.at[:, part], sems.at[1 + piece]))
     copies.append(pltpu.make_async_copy(table_hbm, table, sems.at[5]))
+    copies.append(pltpu.make_async_copy(pairs_hbm, pairs_out, sems.at[6]))
     for copy in copies:
         copy.start()
     copies[0].wait()
@@ -202,6 +203,7 @@
     first_steps(filt, rows, 0, HALF, high, low, 0)
     first_steps(filt, rows, HALF, len(plan) - HALF, more_high, more_low, 0)
     copies[5].wait()
+    copies[6].wait()
     second_steps(table, high, low, turned, ready, out_ref, 0, out_sems)
 
 
@@ -233,28 +235,30 @@
     ]
 
 
-def middle_call(plan, own, keep, volts, taps, table):
+def middle_call(plan, own, tile_pairs, volts, taps, table):
     rows, fft_len = volts.shape[0], taps.shape[1]
     cols = HALF * rows
     more = jax.ShapeDtypeStruct((RADIX // 2, (len(plan) - HALF) * rows, 2 * LANES), jnp.bfloat16)
     partial = jax.ShapeDtypeStruct((len(own) * rows, fft_len), jnp.float32)
     hbm = pl.BlockSpec(memory_space=pltpu.HBM)
     vmem = pl.BlockSpec(memory_space=pltpu.VMEM)
+    smem = pl.BlockSpec(memory_space=pltpu.SMEM)
     return pl.pallas_call(
         functools.partial(middle_kernel, plan, own, fft_len),
         out_shape=(
             pltpu.HBM((fft_len, 2 * cols), jnp.bfloat16),
             *(pltpu.VMEM(x.shape, x.dtype) for x in (more, more, partial, taps, table)),
+            pltpu.SMEM(tile_pairs.shape, tile_pairs.dtype),
         ),
-        in_specs=[pl.BlockSpec(memory_space=pltpu.SMEM), hbm, hbm, hbm],
-        out_specs=(hbm, vmem, vmem, vmem, vmem, vmem),
+        in_specs=[hbm, hbm, hbm, hbm],
+        out_specs=(hbm, vmem, vmem, vmem, vmem, vmem, smem),
         scratch_shapes=[pltpu.VMEM(volts.shape, volts.dtype)]
         + spectra_scratch(rows, fft_len, len(plan))
-        + [pltpu.SemaphoreType.DMA((6,))],
+        + [pltpu.SemaphoreType.DMA((7,))],
         compiler_params=pltpu.CompilerParams(vmem_limit_bytes=VMEM_LIMIT),
         cost_estimate=pl.CostEstimate(flops=10**9, bytes_accessed=8 * 2**20, transcendentals=0),
         name="middle",
-    )(keep, *(pltpu.with_memory_space_constraint(x, pltpu.HBM) for x in (volts, taps, table)))
+    )(*(pltpu.with_memory_space_constraint(x, pltpu.HBM) for x in (tile_pairs, volts, taps, table)))
 
 
 def edge_call(plan, taps, table, earlier, later, partial, more_high, more_low, spectra):
@@ -340,11 +344,11 @@
                 for part in range(2):
                     col = part * stations + second * TILE
                     tiles[chan, first, second, part] = sums[first * TILE : (first + 1) * TILE, col : col + TILE] * scale
-        for tile in range(pairs_ref.shape[0]):
+        for tile in range(pairs_ref.shape[1]):
             for part in range(2):
                 copies.append(
                     pltpu.make_async_copy(
-                        tiles.at[chan, pairs_ref[tile, 0], pairs_ref[tile, 1], part],
+                        tiles.at[chan, pairs_ref[0, tile], pairs_ref[1, tile], part],
                         out_ref.at[part, chan, tile],
                         sems.at[len(copies)],
                     )
@@ -358,7 +362,7 @@
     rows, lanes = got.shape
     stations = 2 * TILE
     depth = 8 * LANES
-    tiles = tile_pairs.shape[0]
+    tiles = tile_pairs.shape[1]
     return pl.pallas_call(
         functools.partial(gram_kernel, 1.0 / total_spectra),
         out_shape=jax.ShapeDtypeStruct((2, chans, tiles, TILE, TILE), jnp.float32),
@@ -404,8 +408,7 @@
     later = lax.ppermute(first, "tm", [(i, (i - 1) % peers) for i in range(peers)])
     table = jnp.asarray(second_step_table(fft_len))
     middle, own, others = plans(frames, tap_count)
-    keep = (lax.axis_index("tm") != peers - 1).astype(jnp.int32).reshape(1)
-    spectra, more_high, more_low, partial, taps, table = middle_call(middle, own, keep, volts, taps, table)
+    spectra, more_high, more_low, partial, taps, table, pairs = middle_call(middle, own, tile_pairs.T, volts, taps, table)
     spectra = edge_call(others, taps, table, earlier, later, partial, more_high, more_low, spectra)
     order = device_order()
     chans = fft_len // 2 // len(order)
@@ -413,7 +416,7 @@
     got = lax.all_to_all(
         blocks, ("stn", "tm"), split_axis=0, concat_axis=0, tiled=True, axis_index_groups=[order]
     )
-    return gram_call(got.reshape(spectra.shape), tile_pairs, chans, frames * peers)
+    return gram_call(got.reshape(spectra.shape), pairs, chans, frames * peers)
 
 
 def solution(mesh):

time: 90 us -> 89.4 us (level)
  blocking collectives: 0 us -> 64.4 us
  waiting for transfers between devices: 52.4 us -> 0.01 us
  starting transfers between devices: 20.9 us -> 8.99 us
    all_to_all x0 -> x1, blocking collectives: none -> 64.4 us  [shards(): lax.all_to_all(blocks, ('stn', 'tm'), split_axis=0, concat_axis=0, tiled=...]
    all_to_all x1 -> x0, waiting for transfers between devices: 52.4 us -> none  [shards(): lax.all_to_all(blocks, ('stn', 'tm'), split_axis=0, concat_axis=0, tiled=...]
    all_to_all x1 -> x0, starting transfers between devices: 11.9 us -> none  [shards(): lax.all_to_all(blocks, ('stn', 'tm'), split_axis=0, concat_axis=0, tiled=...]
  transfers between devices with their start and end apart: 3 -> 2, of which waited for: 1 -> 0; matrix products, arithmetic and copies ran while one was open for 0% -> 0% of each run, Pallas kernels for 10% -> 10%
where the time goes in v6:
time: 89.4 us; the launch traced here: 89.2 us
  blocking collectives  64.4 us (72%)
  Pallas kernels  15.8 us (18%)
  starting transfers between devices  8.99 us (10%)
    all_to_all x1, blocking collectives, shards(): lax.all_to_all(blocks, ('stn', 'tm'), split_axis=0, concat_axis=0, tiled=...  64.4 us
    pallas_call x1, Pallas kernels, middle_call(): pl.pallas_call(functools.partial(middle_kernel, plan, own, fft_len), out_...  8.59 us
    ppermute x1, starting transfers between devices, shards(): lax.ppermute(first, 'tm', [(i, (i - 1) % peers) for i in range(peers)])  4.94 us
    ppermute x1, starting transfers between devices, shards(): earlier = lax.ppermute(last, 'tm', [(i, i + 1) for i in range(peers - 1)])  4.05 us
    pallas_call x1, Pallas kernels, edge_call(): pl.pallas_call(functools.partial(edge_kernel, plan, fft_len), out_shape=p...  3.25 us
    pallas_call x1, Pallas kernels, gram_call(): pl.pallas_call(functools.partial(gram_kernel, 1.0 / total_spectra), out_s...  2.88 us
  transfers between devices with their start and end apart: 2, of which 0 were waited for; matrix products, arithmetic and copies ran while one was open for 0% of the time, Pallas kernels for 10%

profile of v6, /device:TPU:1, one launch (start us, length us, event | category | flops | bytes accessed | tf_op | source)
XLA Modules:
  0.0 89.2 jit_solution(5298195317346681175)
XLA Ops:
  0.0 1.1 %ends.1 = (bf16[16,12288]{1,0:T(8,128)(2,1)S(1)}, bf16[16,10240]{1,0:T(8,128)(2,1)S(1)}) custom-call(bf16[16,65536]{1,0:T(8,128)(2,1)} %volts.1), custom_call_target="tpu_custom_call" | custom-call | tf_op jit(solution)/shard_map/ends/pallas_call | solution.py:299
  1.1 4.1 %collective-permute-start = (bf16[16,12288]{1,0:T(8,128)(2,1)S(1)}, bf16[16,12288]{1,0:T(8,128)(2,1)S(1)}, u32[]{:S(2)}, u32[]{:S(2)}) collective-permute-start(bf16[16,12288]{1,0:T(8,128)(2,1)S(1)} %get-tuple-element.17), channel_id=1, source_target_pairs={{0,1},{1,2},{2,3},{3,4},{4,5},{5,6},{6,7},{7,8},{8,9},{9,10},{10,1... | collective-permute-start | bytes 1179656 | tf_op jit(solution)/shard_map/ppermute | solution.py:407
  5.2 4.9 %collective-permute-start.1 = (bf16[16,10240]{1,0:T(8,128)(2,1)S(1)}, bf16[16,10240]{1,0:T(8,128)(2,1)S(1)}, u32[]{:S(2)}, u32[]{:S(2)}) collective-permute-start(bf16[16,10240]{1,0:T(8,128)(2,1)S(1)} %get-tuple-element.18), channel_id=1, source_target_pairs={{0,15},{1,0},{2,1},{3,2},{4,3},{5,4},{6,5},{7,6},{8,7},{9,8},{10,9... | collective-permute-start | bytes 983048 | tf_op jit(solution)/shard_map/ppermute | solution.py:408
  10.1 8.6 %middle.1 = (bf16[2048,512]{1,0:T(8,128)(2,1)}, bf16[8,80,256]{2,1,0:T(8,128)(2,1)S(1)}, bf16[8,80,256]{2,1,0:T(8,128)(2,1)S(1)}, f32[176,2048]{1,0:T(8,128)S(1)...) custom-call(s32[2,3]{1,0:T(2,128)} %bitcast.5, bf16[16,65536]{1,0:T(8,128)(2,1)} %volts.1, ...), custom_call_target="tpu_custom_call" | custom-call | flops 1000000000 | bytes 8388608 | tf_op jit(solution)/shard_map/middle/pallas_call | solution.py:246
  18.7 0.0 collective-permute-done.1.later
  18.7 0.0 collective-permute-done.earlier
  18.7 3.3 %edge.1 = bf16[2048,512]{1,0:T(8,128)(2,1)} custom-call(f32[12,2048]{1,0:T(8,128)S(1)} %get-tuple-element.15.taps, bf16[8,512,256]{2,1,0:T(8,128)(2,1)S(1)} %get-tuple-element.16.table, bf16[16,12288]{1,0:T(8,128)(2,1)S(1)} %collective-permute-done.earlier, bf16[16,10240]{1,0:T(8,128)(2,1)S(1)} %collective-permute-done.1.later, ...), custom_call_target="tpu_custom_call", output_to_operand_aliasing={{}: (7, {})} | custom-call | flops 1000000000 | bytes 8388608 | tf_op jit(solution)/shard_map/edge/pallas_call | solution.py:269
  22.0 64.4 %all_to_all.5 = bf16[256,8,512]{2,1,0:T(8,128)(2,1)S(1)} all-to-all(bf16[256,8,512]{2,1,0:T(8,128)(2,1)} %bitcast.4), channel_id=1, replica_groups={{0,128,8,136,4,132,12,140,1,129,9,137,5,133,13,141,2,130,10,138,6,134,1..., dimensions={0} | all-to-all | bytes 4194304 | tf_op jit(solution)/shard_map/all_to_all | solution.py:416
  86.3 2.9 %grams.1 = f32[2,4,3,128,128]{4,3,2,1,0:T(8,128)} custom-call(s32[2,3]{1,0:T(2,128)S(4)} %get-tuple-element.14.pairs_ref, bf16[2048,512]{1,0:T(8,128)(2,1)S(1)} %bitcast.3), custom_call_target="tpu_custom_call" | custom-call | tf_op jit(solution)/shard_map/grams/pallas_call | solution.py:366
Async XLA Ops:
  1.1 17.6 %collective-permute-start = (bf16[16,12288]{1,0:T(8,128)(2,1)S(1)}, bf16[16,12288]{1,0:T(8,128)(2,1)S(1)}, u32[]{:S(2)}, u32[]{:S(2)}) collective-permute-start(bf16[16,12288]{1,0:T(8,128)(2,1)S(1)} %get-tuple-element.17), channel_id=1, source_target_pairs={{0,1},{1,2},{2,3},{3,4},{4,5},{5,6},{6,7},{7,8},{8,9},{9,10},{10,1... | collective-permute-start | bytes 1179656 | tf_op jit(solution)/shard_map/ppermute | solution.py:407
  5.2 13.5 %collective-permute-start.1 = (bf16[16,10240]{1,0:T(8,128)(2,1)S(1)}, bf16[16,10240]{1,0:T(8,128)(2,1)S(1)}, u32[]{:S(2)}, u32[]{:S(2)}) collective-permute-start(bf16[16,10240]{1,0:T(8,128)(2,1)S(1)} %get-tuple-element.18), channel_id=1, source_target_pairs={{0,15},{1,0},{2,1},{3,2},{4,3},{5,4},{6,5},{7,6},{8,7},{9,8},{10,9... | collective-permute-start | bytes 983048 | tf_op jit(solution)/shard_map/ppermute | solution.py:408

commit v7 on v6

--- a/solution.py
+++ b/solution.py
@@ -171,11 +171,11 @@
                         turned[lane, pl.ds(row, z_size, stride=block), :] = result[
                             first : first + z_size, lane * LANES : (lane + 1) * LANES
                         ]
+        if pair == 3:
+            copies += send(0, 1, 0)
         if pair == 4:
-            copies += send(0, 1, 0) + send(3, 1, PLANE)
-    copies += send(1, 2, 2 * PLANE)
-    for copy in copies:
-        copy.wait()
+            copies += send(3, 1, PLANE)
+    return copies + send(1, 2, 2 * PLANE)
 
 
 def middle_kernel(plan, own, fft_len, pairs_hbm, volts_hbm, taps_hbm, table_hbm, out_ref, more_high, more_low,
@@ -199,12 +199,13 @@
         upto = bounds[piece + 1] - (taps.shape[0] - 1)
         filter_outputs(plan[done:upto], fft_len, keep, [volts], taps, None, filt, done)
         done = upto
+    first_steps(filt, rows, 0, HALF, high, low, 0)
+    copies[5].wait()
+    sent = second_steps(table, high, low, turned, ready, out_ref, 0, out_sems)
     filter_outputs(own, fft_len, keep, [volts], taps, None, partial, 0)
-    first_steps(filt, rows, 0, HALF, high, low, 0)
     first_steps(filt, rows, HALF, len(plan) - HALF, more_high, more_low, 0)
-    copies[5].wait()
-    copies[6].wait()
-    second_steps(table, high, low, turned, ready, out_ref, 0, out_sems)
+    for copy in [copies[6], *sent]:
+        copy.wait()
 
 
 def edge_kernel(plan, fft_len, taps, table, earlier, later, partial, more_high, more_low, _, out_ref,
@@ -220,7 +221,8 @@
     first_steps(filt, rows, 0, len(plan), high, low, more_high.shape[1], len(plan))
     for copy in copies:
         copy.wait()
-    second_steps(table, high, low, turned, ready, out_ref, 1, out_sems)
+    for copy in second_steps(table, high, low, turned, ready, out_ref, 1, out_sems):
+        copy.wait()
 
 
 def spectra_scratch(rows, fft_len, outputs):

time: 89.4 us -> 89.4 us (level)
  transfers between devices with their start and end apart: 2 -> 2, of which waited for: 0 -> 0; matrix products, arithmetic and copies ran while one was open for 0% -> 0% of each run, Pallas kernels for 10% -> 9%
where the time goes in v7:
time: 89.4 us; the launch traced here: 89.2 us
  blocking collectives  65.1 us (73%)
  Pallas kernels  15.1 us (17%)
  starting transfers between devices  8.99 us (10%)
    all_to_all x1, blocking collectives, shards(): lax.all_to_all(blocks, ('stn', 'tm'), split_axis=0, concat_axis=0, tiled=...  65.1 us
    pallas_call x1, Pallas kernels, middle_call(): pl.pallas_call(functools.partial(middle_kernel, plan, own, fft_len), out_...  7.83 us
    ppermute x1, starting transfers between devices, shards(): lax.ppermute(first, 'tm', [(i, (i - 1) % peers) for i in range(peers)])  4.94 us
    ppermute x1, starting transfers between devices, shards(): earlier = lax.ppermute(last, 'tm', [(i, i + 1) for i in range(peers - 1)])  4.05 us
    pallas_call x1, Pallas kernels, edge_call(): pl.pallas_call(functools.partial(edge_kernel, plan, fft_len), out_shape=p...  3.25 us
    pallas_call x1, Pallas kernels, gram_call(): pl.pallas_call(functools.partial(gram_kernel, 1.0 / total_spectra), out_s...  2.89 us
  transfers between devices with their start and end apart: 2, of which 0 were waited for; matrix products, arithmetic and copies ran while one was open for 0% of the time, Pallas kernels for 9%

profile of v7, /device:TPU:1, one launch (start us, length us, event | category | flops | bytes accessed | tf_op | source)
XLA Modules:
  0.0 89.2 jit_solution(4740119345945949692)
XLA Ops:
  0.0 1.1 %ends.1 = (bf16[16,12288]{1,0:T(8,128)(2,1)S(1)}, bf16[16,10240]{1,0:T(8,128)(2,1)S(1)}) custom-call(bf16[16,65536]{1,0:T(8,128)(2,1)} %volts.1), custom_call_target="tpu_custom_call" | custom-call | tf_op jit(solution)/shard_map/ends/pallas_call | solution.py:301
  1.1 4.1 %collective-permute-start = (bf16[16,12288]{1,0:T(8,128)(2,1)S(1)}, bf16[16,12288]{1,0:T(8,128)(2,1)S(1)}, u32[]{:S(2)}, u32[]{:S(2)}) collective-permute-start(bf16[16,12288]{1,0:T(8,128)(2,1)S(1)} %get-tuple-element.17), channel_id=1, source_target_pairs={{0,1},{1,2},{2,3},{3,4},{4,5},{5,6},{6,7},{7,8},{8,9},{9,10},{10,1... | collective-permute-start | bytes 1179656 | tf_op jit(solution)/shard_map/ppermute | solution.py:409
  5.2 4.9 %collective-permute-start.1 = (bf16[16,10240]{1,0:T(8,128)(2,1)S(1)}, bf16[16,10240]{1,0:T(8,128)(2,1)S(1)}, u32[]{:S(2)}, u32[]{:S(2)}) collective-permute-start(bf16[16,10240]{1,0:T(8,128)(2,1)S(1)} %get-tuple-element.18), channel_id=1, source_target_pairs={{0,15},{1,0},{2,1},{3,2},{4,3},{5,4},{6,5},{7,6},{8,7},{9,8},{10,9... | collective-permute-start | bytes 983048 | tf_op jit(solution)/shard_map/ppermute | solution.py:410
  10.1 7.8 %middle.1 = (bf16[2048,512]{1,0:T(8,128)(2,1)}, bf16[8,80,256]{2,1,0:T(8,128)(2,1)S(1)}, bf16[8,80,256]{2,1,0:T(8,128)(2,1)S(1)}, f32[176,2048]{1,0:T(8,128)S(1)...) custom-call(s32[2,3]{1,0:T(2,128)} %bitcast.5, bf16[16,65536]{1,0:T(8,128)(2,1)} %volts.1, ...), custom_call_target="tpu_custom_call" | custom-call | flops 1000000000 | bytes 8388608 | tf_op jit(solution)/shard_map/middle/pallas_call | solution.py:248
  18.0 0.0 collective-permute-done.1.later
  18.0 0.0 collective-permute-done.earlier
  18.0 3.3 %edge.1 = bf16[2048,512]{1,0:T(8,128)(2,1)} custom-call(f32[12,2048]{1,0:T(8,128)S(1)} %get-tuple-element.15.taps, bf16[8,512,256]{2,1,0:T(8,128)(2,1)S(1)} %get-tuple-element.16.table, bf16[16,12288]{1,0:T(8,128)(2,1)S(1)} %collective-permute-done.earlier, bf16[16,10240]{1,0:T(8,128)(2,1)S(1)} %collective-permute-done.1.later, ...), custom_call_target="tpu_custom_call", output_to_operand_aliasing={{}: (7, {})} | custom-call | flops 1000000000 | bytes 8388608 | tf_op jit(solution)/shard_map/edge/pallas_call | solution.py:271
  21.2 65.1 %all_to_all.5 = bf16[256,8,512]{2,1,0:T(8,128)(2,1)S(1)} all-to-all(bf16[256,8,512]{2,1,0:T(8,128)(2,1)} %bitcast.4), channel_id=1, replica_groups={{0,128,8,136,4,132,12,140,1,129,9,137,5,133,13,141,2,130,10,138,6,134,1..., dimensions={0} | all-to-all | bytes 4194304 | tf_op jit(solution)/shard_map/all_to_all | solution.py:418
  86.4 2.9 %grams.1 = f32[2,4,3,128,128]{4,3,2,1,0:T(8,128)} custom-call(s32[2,3]{1,0:T(2,128)S(4)} %get-tuple-element.14.pairs_ref, bf16[2048,512]{1,0:T(8,128)(2,1)S(1)} %bitcast.3), custom_call_target="tpu_custom_call" | custom-call | tf_op jit(solution)/shard_map/grams/pallas_call | solution.py:368
Async XLA Ops:
  1.1 16.9 %collective-permute-start = (bf16[16,12288]{1,0:T(8,128)(2,1)S(1)}, bf16[16,12288]{1,0:T(8,128)(2,1)S(1)}, u32[]{:S(2)}, u32[]{:S(2)}) collective-permute-start(bf16[16,12288]{1,0:T(8,128)(2,1)S(1)} %get-tuple-element.17), channel_id=1, source_target_pairs={{0,1},{1,2},{2,3},{3,4},{4,5},{5,6},{6,7},{7,8},{8,9},{9,10},{10,1... | collective-permute-start | bytes 1179656 | tf_op jit(solution)/shard_map/ppermute | solution.py:409
  5.2 12.8 %collective-permute-start.1 = (bf16[16,10240]{1,0:T(8,128)(2,1)S(1)}, bf16[16,10240]{1,0:T(8,128)(2,1)S(1)}, u32[]{:S(2)}, u32[]{:S(2)}) collective-permute-start(bf16[16,10240]{1,0:T(8,128)(2,1)S(1)} %get-tuple-element.18), channel_id=1, source_target_pairs={{0,15},{1,0},{2,1},{3,2},{4,3},{5,4},{6,5},{7,6},{8,7},{9,8},{10,9... | collective-permute-start | bytes 983048 | tf_op jit(solution)/shard_map/ppermute | solution.py:410

commit v8 on v7

--- a/solution.py
+++ b/solution.py
@@ -18,6 +18,7 @@
 HALF = 16
 Z_HIGH, PLANE, Z_LOW, Y_SIZE = 2, 8, 4, 4
 Z_LOW_ORDER = (0, 2, 1, 3)
+ENDS_PIECE = 4096
 VMEM_LIMIT = 48 * 1024 * 1024
 
 
@@ -284,11 +285,15 @@
 
 
 def ends_kernel(volts, last_ref, first_ref, sems):
-    size = last_ref.shape[1]
-    copies = [
-        pltpu.make_async_copy(volts.at[:, pl.ds(volts.shape[1] - size, size)], last_ref, sems.at[0]),
-        pltpu.make_async_copy(volts.at[:, pl.ds(0, first_ref.shape[1])], first_ref, sems.at[1]),
-    ]
+    copies = []
+    for ref, start in ((last_ref, volts.shape[1] - last_ref.shape[1]), (first_ref, 0)):
+        for piece in range(0, ref.shape[1], ENDS_PIECE):
+            size = min(ENDS_PIECE, ref.shape[1] - piece)
+            copies.append(
+                pltpu.make_async_copy(
+                    volts.at[:, pl.ds(start + piece, size)], ref.at[:, pl.ds(piece, size)], sems.at[len(copies)]
+                )
+            )
     for copy in copies:
         copy.start()
     for copy in copies:
@@ -303,7 +308,7 @@
         out_shape=(pltpu.VMEM((rows, last), volts.dtype), pltpu.VMEM((rows, first), volts.dtype)),
         in_specs=[pl.BlockSpec(memory_space=pltpu.HBM)],
         out_specs=(vmem, vmem),
-        scratch_shapes=[pltpu.SemaphoreType.DMA((2,))],
+        scratch_shapes=[pltpu.SemaphoreType.DMA((-(-last // ENDS_PIECE) - (-first // ENDS_PIECE),))],
         name="ends",
     )(pltpu.with_memory_space_constraint(volts, pltpu.HBM))
 

time: 89.4 us -> 89.5 us (level)
  no operation moved by 1% of the time
where the time goes in v8:
time: 89.5 us; the launch traced here: 89.3 us
  blocking collectives  65.1 us (73%)
  Pallas kernels  15.2 us (17%)
  starting transfers between devices  8.99 us (10%)
    all_to_all x1, blocking collectives, shards(): lax.all_to_all(blocks, ('stn', 'tm'), split_axis=0, concat_axis=0, tiled=...  65.1 us
    pallas_call x1, Pallas kernels, middle_call(): pl.pallas_call(functools.partial(middle_kernel, plan, own, fft_len), out_...  7.83 us
    ppermute x1, starting transfers between devices, shards(): lax.ppermute(first, 'tm', [(i, (i - 1) % peers) for i in range(peers)])  4.94 us
    ppermute x1, starting transfers between devices, shards(): earlier = lax.ppermute(last, 'tm', [(i, i + 1) for i in range(peers - 1)])  4.05 us
    pallas_call x1, Pallas kernels, edge_call(): pl.pallas_call(functools.partial(edge_kernel, plan, fft_len), out_shape=p...  3.25 us
    pallas_call x1, Pallas kernels, gram_call(): pl.pallas_call(functools.partial(gram_kernel, 1.0 / total_spectra), out_s...  2.88 us
  transfers between devices with their start and end apart: 2, of which 0 were waited for; matrix products, arithmetic and copies ran while one was open for 0% of the time, Pallas kernels for 9%

profile of v8, /device:TPU:1, one launch (start us, length us, event | category | flops | bytes accessed | tf_op | source)
XLA Modules:
  0.0 89.3 jit_solution(4373432065065388813)
XLA Ops:
  0.0 1.2 %ends.1 = (bf16[16,12288]{1,0:T(8,128)(2,1)S(1)}, bf16[16,10240]{1,0:T(8,128)(2,1)S(1)}) custom-call(bf16[16,65536]{1,0:T(8,128)(2,1)} %volts.1), custom_call_target="tpu_custom_call" | custom-call | tf_op jit(solution)/shard_map/ends/pallas_call | solution.py:306
  1.2 4.1 %collective-permute-start = (bf16[16,12288]{1,0:T(8,128)(2,1)S(1)}, bf16[16,12288]{1,0:T(8,128)(2,1)S(1)}, u32[]{:S(2)}, u32[]{:S(2)}) collective-permute-start(bf16[16,12288]{1,0:T(8,128)(2,1)S(1)} %get-tuple-element.17), channel_id=1, source_target_pairs={{0,1},{1,2},{2,3},{3,4},{4,5},{5,6},{6,7},{7,8},{8,9},{9,10},{10,1... | collective-permute-start | bytes 1179656 | tf_op jit(solution)/shard_map/ppermute | solution.py:414
  5.3 4.9 %collective-permute-start.1 = (bf16[16,10240]{1,0:T(8,128)(2,1)S(1)}, bf16[16,10240]{1,0:T(8,128)(2,1)S(1)}, u32[]{:S(2)}, u32[]{:S(2)}) collective-permute-start(bf16[16,10240]{1,0:T(8,128)(2,1)S(1)} %get-tuple-element.18), channel_id=1, source_target_pairs={{0,15},{1,0},{2,1},{3,2},{4,3},{5,4},{6,5},{7,6},{8,7},{9,8},{10,9... | collective-permute-start | bytes 983048 | tf_op jit(solution)/shard_map/ppermute | solution.py:415
  10.2 7.8 %middle.1 = (bf16[2048,512]{1,0:T(8,128)(2,1)}, bf16[8,80,256]{2,1,0:T(8,128)(2,1)S(1)}, bf16[8,80,256]{2,1,0:T(8,128)(2,1)S(1)}, f32[176,2048]{1,0:T(8,128)S(1)...) custom-call(s32[2,3]{1,0:T(2,128)} %bitcast.5, bf16[16,65536]{1,0:T(8,128)(2,1)} %volts.1, ...), custom_call_target="tpu_custom_call" | custom-call | flops 1000000000 | bytes 8388608 | tf_op jit(solution)/shard_map/middle/pallas_call | solution.py:249
  18.1 0.0 collective-permute-done.1.later
  18.1 0.0 collective-permute-done.earlier
  18.1 3.3 %edge.1 = bf16[2048,512]{1,0:T(8,128)(2,1)} custom-call(f32[12,2048]{1,0:T(8,128)S(1)} %get-tuple-element.15.taps, bf16[8,512,256]{2,1,0:T(8,128)(2,1)S(1)} %get-tuple-element.16.table, bf16[16,12288]{1,0:T(8,128)(2,1)S(1)} %collective-permute-done.earlier, bf16[16,10240]{1,0:T(8,128)(2,1)S(1)} %collective-permute-done.1.later, ...), custom_call_target="tpu_custom_call", output_to_operand_aliasing={{}: (7, {})} | custom-call | flops 1000000000 | bytes 8388608 | tf_op jit(solution)/shard_map/edge/pallas_call | solution.py:272
  21.3 65.1 %all_to_all.5 = bf16[256,8,512]{2,1,0:T(8,128)(2,1)S(1)} all-to-all(bf16[256,8,512]{2,1,0:T(8,128)(2,1)} %bitcast.4), channel_id=1, replica_groups={{0,128,8,136,4,132,12,140,1,129,9,137,5,133,13,141,2,130,10,138,6,134,1..., dimensions={0} | all-to-all | bytes 4194304 | tf_op jit(solution)/shard_map/all_to_all | solution.py:423
  86.5 2.9 %grams.1 = f32[2,4,3,128,128]{4,3,2,1,0:T(8,128)} custom-call(s32[2,3]{1,0:T(2,128)S(4)} %get-tuple-element.14.pairs_ref, bf16[2048,512]{1,0:T(8,128)(2,1)S(1)} %bitcast.3), custom_call_target="tpu_custom_call" | custom-call | tf_op jit(solution)/shard_map/grams/pallas_call | solution.py:373
Async XLA Ops:
  1.2 16.9 %collective-permute-start = (bf16[16,12288]{1,0:T(8,128)(2,1)S(1)}, bf16[16,12288]{1,0:T(8,128)(2,1)S(1)}, u32[]{:S(2)}, u32[]{:S(2)}) collective-permute-start(bf16[16,12288]{1,0:T(8,128)(2,1)S(1)} %get-tuple-element.17), channel_id=1, source_target_pairs={{0,1},{1,2},{2,3},{3,4},{4,5},{5,6},{6,7},{7,8},{8,9},{9,10},{10,1... | collective-permute-start | bytes 1179656 | tf_op jit(solution)/shard_map/ppermute | solution.py:414
  5.3 12.8 %collective-permute-start.1 = (bf16[16,10240]{1,0:T(8,128)(2,1)S(1)}, bf16[16,10240]{1,0:T(8,128)(2,1)S(1)}, u32[]{:S(2)}, u32[]{:S(2)}) collective-permute-start(bf16[16,10240]{1,0:T(8,128)(2,1)S(1)} %get-tuple-element.18), channel_id=1, source_target_pairs={{0,15},{1,0},{2,1},{3,2},{4,3},{5,4},{6,5},{7,6},{8,7},{9,8},{10,9... | collective-permute-start | bytes 983048 | tf_op jit(solution)/shard_map/ppermute | solution.py:415
